TPU v7x, 512 devices: a whole 4x8x8 slice. The times are simulated.
512 devices in a mesh: inp: 128 (over y, z, core), sec: 4 (over x).
Axes of the slice: x: 4, y: 8, z: 8, core: 2. Of those that a mesh axis runs over, the one named last changes fastest.
Arguments:
- samples: bfloat16 [1024, 128, 2048], P('inp', 'sec'), may hold values from -6 to 6
- fir_weights: float32 [4, 2048], replicated, may hold values from -3 to 3
- channel_owner: int32 [768], replicated, may hold values from 0 to 127, as said below
Outputs:
- visibility: bfloat16 [1024, 1024, 1024], P(('inp', 'sec'))
- auto_power: float32 [1024, 1024], P(('inp', 'sec'))
Inputs may be any that keep to these rules, and one draw needn't show every extreme that they name: `channel_owner`: no owner is named by more than 8 channels, and some owner is named by exactly 8; counts differ from owner to owner.
All inputs are finite; a program needn't handle non-finite values.
Results may differ from a plain program's by a relative error of at most 0.0076.
Values may be sent and summed in bfloat16 or wider, within the bound.
No kernel may reach another device: no remote copies, remote signals or barrier semaphores. Data moves between devices by JAX's collectives and lax.ppermute only.
A program may use at most 64 MiB of HBM per device.

v0:
```python
import math

import jax
import jax.numpy as jnp
from jax import lax
from jax.sharding import PartitionSpec as P

POINTS = 2048
CHANNELS = 768
TAPS = 4
FRAMES = 128


def passed_along(value, axis, by):
    length = lax.axis_size(axis)
    pairs = [(i, i + by) for i in range(length) if 0 <= i + by < length]
    return lax.ppermute(value, axis, pairs)


def dft_table():
    sample_index = jnp.arange(POINTS, dtype=jnp.int32)
    channel_bins = jnp.arange(CHANNELS, dtype=jnp.int32)
    phases = sample_index[:, None] * channel_bins[None, :] % POINTS
    angles = phases.astype(jnp.float32) * (2.0 * math.pi / POINTS)
    norm_factor = 1.0 / math.sqrt(POINTS)
    return (jnp.concatenate([jnp.cos(angles), -jnp.sin(angles)], axis=1) * norm_factor).astype(
        jnp.bfloat16
    )


def slot_lookup(channel_owner, slot_total, slots_per):
    channel_index = jnp.arange(channel_owner.shape[0], dtype=jnp.int32)
    earlier_same = (channel_owner[:, None] == channel_owner[None, :]) & (
        channel_index[None, :] < channel_index[:, None]
    )
    slot_rank = jnp.sum(earlier_same.astype(jnp.int32), axis=1)
    slot_target = channel_owner * slots_per + slot_rank
    slot_index = jnp.arange(slot_total, dtype=jnp.int32)
    slot_match = (slot_target[None, :] == slot_index[:, None]).astype(jnp.int32)
    channel_id = jnp.sum(slot_match * channel_index[None, :], axis=1)
    slot_live = jnp.sum(slot_match, axis=1)
    return (channel_id, slot_live)


def cross_terms(received):
    twisted = jnp.stack([received[:, 1], -received[:, 0]], axis=1)
    full_width = received.shape[-1]
    real_vis = jnp.einsum("sktr,sktj->srj", received, received, preferred_element_type=jnp.float32)
    imag_vis = jnp.einsum("sktr,sktj->srj", twisted, received, preferred_element_type=jnp.float32)
    row_index = jnp.arange(full_width)
    upper_mask = row_index[:, None] <= row_index[None, :]
    return jnp.where(upper_mask[None], real_vis, imag_vis)


def local(samples, fir_weights, channel_owner):
    in_dev, frame_dev, points = samples.shape
    owners_count = lax.axis_size("inp")
    slots_per = 4 * CHANNELS // (3 * owners_count)
    last_frames = samples[:, frame_dev - (TAPS - 1) :, :]
    previous = passed_along(last_frames, "sec", 1)
    extended = jnp.concatenate([previous, samples], axis=1)
    accumulated = jnp.zeros((in_dev, frame_dev, points), jnp.float32)
    for tap in range(TAPS):
        offset = TAPS - 1 - tap
        accumulated = accumulated + fir_weights[tap][None, None, :] * extended[
            :, offset : offset + frame_dev, :
        ].astype(jnp.float32)
    filtered = accumulated.astype(jnp.bfloat16)
    spectra = jnp.dot(
        filtered.reshape(in_dev * frame_dev, points),
        dft_table(),
        preferred_element_type=jnp.float32,
    ).astype(jnp.bfloat16)
    channel_id, slot_live = slot_lookup(channel_owner, owners_count * slots_per, slots_per)
    pick_index = jnp.concatenate([channel_id, channel_id + CHANNELS])
    is_live = jnp.concatenate([slot_live, slot_live]) > 0
    picked = jnp.where(
        is_live[None, :], jnp.take(spectra, pick_index, axis=1), jnp.zeros((), jnp.bfloat16)
    )
    buffer = picked.reshape(in_dev, frame_dev, 2, owners_count, slots_per).transpose(3, 4, 2, 1, 0)
    received = lax.all_to_all(
        lax.all_to_all(buffer, "inp", split_axis=0, concat_axis=4, tiled=True),
        "sec",
        split_axis=1,
        concat_axis=3,
        tiled=True,
    )
    received = received[0]
    packed = cross_terms(received)
    visibility = (packed / FRAMES).astype(jnp.bfloat16)
    as_float = received.astype(jnp.float32)
    auto_power = jnp.sum(as_float * as_float, axis=(1, 2)) / FRAMES
    return (visibility, auto_power)


def solution(mesh):
    in_specs = (P("inp", "sec", None), P(), P())
    out_specs = (P(("inp", "sec"), None, None), P(("inp", "sec"), None))
    return jax.shard_map(local, mesh=mesh, in_specs=in_specs, out_specs=out_specs, check_vma=False)
```

profile of v0, /device:TPU:1, one launch (start us, length us, event | category | flops | bytes accessed | tf_op | source)
XLA Modules:
  0.0 152.8 jit_solution(845576131489136494)
XLA Ops:
  0.6 1.0 slice.32
  1.7 4.0 %collective-permute-start = (bf16[8,3,2048]{2,1,0:T(4,128)(2,1)S(1)}, bf16[8,3,2048]{2,1,0:T(4,128)(2,1)S(1)}, u32[]{:S(2)}, u32[]{:S(2)}) collective-permute-start(bf16[8,3,2048]{2,1,0:T(4,128)(2,1)S(1)} %slice.32), channel_id=1, source_target_pairs={{0,1},{1,2},{2,3},{4,5},{5,6},{6,7},{8,9},{9,10},{10,11},{12,13},{... | collective-permute-start | bytes 294920 | tf_op jit(solution)/shard_map/ppermute | solution.py:17
  5.6 1.1 convert_reduce_fusion.1
  6.7 0.7 multiply_add_fusion
  7.4 1.0 convert_reduce_fusion
  8.4 0.1 concatenate.49
  8.6 0.0 copy-start.1
  8.6 0.0 copy-start
  8.6 26.2 %sine_negate_fusion = (f32[2048,768]{1,0:T(8,128)}, f32[2048,768]{1,0:T(8,128)}) fusion(), kind=kLoop, calls=%fused_computation.12 | loop fusion | flops 23592960 | bytes 12582912 | tf_op jit(solution)/shard_map/neg | solution.py:26
  34.9 0.1 gt.19
  35.1 0.0 copy-done.1
  35.2 0.2 copy.26
  35.4 0.0 collective-permute-done
  35.4 0.0 copy-done
  35.4 1.1 add_convert_fusion
  36.5 6.4 %fusion.12 = bf16[256,1536]{1,0:T(8,128)(2,1)S(1)} fusion(bf16[256,2048]{1,0:T(8,128)(2,1)S(1)} %bitcast.51, f32[2048,768]{1,0:T(8,128)} %get-tuple-element.10, f32[2048,768]{1,0:T(8,128)} %get-tuple-element.11), kind=kOutput, calls=%fused_computation.24 | convolution fusion | flops 1620443136 | bytes 14417920 | tf_op jit(solution)/shard_map/dot_general | solution.py:69
  42.9 0.3 copy.27
  43.2 7.5 %gather_fusion = bf16[2048,256]{1,0:T(8,128)(2,1)S(1)} fusion(bf16[256,1536]{0,1:T(8,128)(2,1)S(1)} %copy.27, s32[2048]{0:T(1024)S(1)} %broadcast_clamp_fusion), kind=kCustom, calls=%fused_computation | custom fusion | bytes 2105344 | tf_op jit(solution)/shard_map/jit(_take)/gather | solution.py:78
  50.7 3.3 %gather.7 = bf16[8,32,2,128,8]{1,0,4,3,2:T(8,128)(2,1)} reshape(bf16[256,2048]{0,1:T(8,128)(2,1)S(1)} %bitcast.50) | data formatting | bytes 2097152 | tf_op jit(solution)/shard_map/jit(_take)/gather | solution.py:78
  54.0 7.5 %copy_bitcast_fusion.1 = bf16[128,2,8,8,32]{4,3,2,1,0:T(8,128)(2,1)} fusion(bf16[8,32,2,128,8]{1,0,4,3,2:T(8,128)(2,1)} %gather.7, pred[2,128,8]{2,1,0:T(8,128)(4,1)S(1)} %copy.26, pred[2,128,8]{2,1,0:T(8,128)(4,1)S(1)} %gt.19), kind=kLoop, calls=%fused_computation.56 | loop fusion | flops 1048576 | bytes 2101248
  61.5 6.5 %reshape.148 = bf16[128,2,2048]{2,1,0:T(2,128)(2,1)S(1)} reshape(bf16[128,2,8,8,32]{4,3,2,1,0:T(8,128)(2,1)} %copy_bitcast_fusion.1) | data formatting | bytes 2097152
  68.1 48.1 %all_to_all.33 = bf16[128,2,2048]{2,1,0:T(2,128)(2,1)S(1)} all-to-all(bf16[128,2,2048]{2,1,0:T(2,128)(2,1)S(1)} %reshape.148), channel_id=1, replica_groups=mesh['inp'=128,'sec'=4] {'inp'}, dimensions={0} | all-to-all | bytes 2097152 | tf_op jit(solution)/shard_map/all_to_all | solution.py:82
  116.2 3.5 %reshape.149 = bf16[128,2,8,8,32]{4,3,2,1,0:T(8,128)(2,1)} reshape(bf16[128,2,2048]{2,1,0:T(2,128)(2,1)S(1)} %all_to_all.33) | data formatting | bytes 2097152
  119.6 5.2 %copy_bitcast_fusion = bf16[1,8,2,32,1024]{3,4,2,1,0:T(8,128)(2,1)} fusion(bf16[128,2,8,8,32]{4,3,2,1,0:T(8,128)(2,1)} %reshape.149), kind=kLoop, calls=%fused_computation.17 | loop fusion | bytes 2097152 | tf_op jit(solution)/shard_map/all_to_all | solution.py:82
  124.8 4.6 %copy.30 = bf16[1,8,2,32,1024]{4,3,2,0,1:T(8,128)(2,1)} copy(bf16[1,8,2,32,1024]{3,4,2,1,0:T(8,128)(2,1)} %copy_bitcast_fusion) | data formatting | bytes 2097152 | tf_op jit(solution)/shard_map/all_to_all | solution.py:82
  129.4 3.7 %all-to-all-start.1 = ((bf16[1,8,2,32,1024]{4,3,2,0,1:T(8,128)(2,1)}), bf16[1,8,2,32,1024]{4,3,2,0,1:T(8,128)(2,1)S(1)}, u32[]{:S(2)}, u32[]{:S(2)}) async-start(bf16[1,8,2,32,1024]{4,3,2,0,1:T(8,128)(2,1)} %copy.30), calls=%async_computation.1 | async-start | bytes 2097152 | tf_op jit(solution)/shard_map/all_to_all | solution.py:81
  133.1 0.3 iota_compare_fusion
  133.4 13.2 %all-to-all-done.1 = bf16[1,8,2,32,1024]{4,3,2,0,1:T(8,128)(2,1)S(1)} async-done(((bf16[1,8,2,32,1024]{4,3,2,0,1:T(8,128)(2,1)}), bf16[1,8,2,32,1024]{4,3,2,0,1:T(8,128)(2,1)S(1)}, u32[]{:S(2)}, u32[]{:S(2)}) %all-to-all-start.1) | async-done | bytes 1048608 | tf_op jit(solution)/shard_map/all_to_all | solution.py:81
  146.6 0.2 multiply_reduce_fusion
  146.9 0.1 copy.31
  147.0 0.1 fusion.24
  147.0 1.3 fusion.26
  148.4 0.6 broadcast_multiply_fusion
  149.0 3.8 %fusion.2 = bf16[2,1024,1024]{2,1,0:T(8,128)(2,1)} fusion(f32[2,1024,1024,1]{2,1,3,0:T(8,128)S(1)} %fusion.26, pred[1024,1024]{1,0:T(8,128)(4,1)S(1)} %iota_compare_fusion, bf16[2,2,128,1024]{3,2,1,0:T(8,128)(2,1)S(1)} %bitcast.47, bf16[2,1,128,1024]{3,2,1,0:T(8,128)(2,1)S(1)} %get-tuple-element.5, bf16[2,1,128,1024]{3,2,1,0:T(8,128)(2,1)S(1)} %get-tuple-element.4), kind=kOutput, calls=%fused_computation.8 | convolution fusion | flops 1080557568 | bytes 15728640 | tf_op jit(solution)/shard_map/sktr,sktj->srj/dot_general | solution.py:49
  (9 shorter events, 0.2 us)
Async XLA Ops:
  1.7 33.7 %collective-permute-start = (bf16[8,3,2048]{2,1,0:T(4,128)(2,1)S(1)}, bf16[8,3,2048]{2,1,0:T(4,128)(2,1)S(1)}, u32[]{:S(2)}, u32[]{:S(2)}) collective-permute-start(bf16[8,3,2048]{2,1,0:T(4,128)(2,1)S(1)} %slice.32), channel_id=1, source_target_pairs={{0,1},{1,2},{2,3},{4,5},{5,6},{6,7},{8,9},{9,10},{10,11},{12,13},{... | collective-permute-start | bytes 294920 | tf_op jit(solution)/shard_map/ppermute | solution.py:17
  8.6 26.5 %copy-start.1 = (f32[4,2048]{1,0:T(4,128)S(1)}, f32[4,2048]{1,0:T(4,128)}, u32[]{:S(2)}) copy-start(f32[4,2048]{1,0:T(4,128)} %param.4) | copy-start | bytes 98308
  8.6 26.7 %copy-start = (bf16[8,32,2048]{2,1,0:T(8,128)(2,1)S(1)}, bf16[8,32,2048]{2,1,0:T(8,128)(2,1)}, u32[]{:S(2)}) copy-start(bf16[8,32,2048]{2,1,0:T(8,128)(2,1)} %param.3) | copy-start | bytes 3145732
  129.4 17.2 %all-to-all-start.1 = ((bf16[1,8,2,32,1024]{4,3,2,0,1:T(8,128)(2,1)}), bf16[1,8,2,32,1024]{4,3,2,0,1:T(8,128)(2,1)S(1)}, u32[]{:S(2)}, u32[]{:S(2)}) async-start(bf16[1,8,2,32,1024]{4,3,2,0,1:T(8,128)(2,1)} %copy.30), calls=%async_computation.1 | async-start | bytes 2097152 | tf_op jit(solution)/shard_map/all_to_all | solution.py:81
where the time goes:
time: 154 us; the launch traced here: 153 us
  blocking collectives  48.1 us (31%)
  other arithmetic  39 us (25%)
  local copies, waits for them, and re-layouts  32.4 us (21%)
  waiting for transfers between devices  13.2 us (9%)
  matrix products  11.5 us (7%)
  starting transfers between devices  7.68 us (5%)
    all_to_all x1, blocking collectives, local(): lax.all_to_all(buffer, 'inp', split_axis=0, concat_axis=4, tiled=True)  48.1 us
    neg x1, other arithmetic, dft_table(): -jnp.sin(angles)  26.2 us
    all_to_all x1, waiting for transfers between devices, local(): lax.all_to_all(lax.all_to_all(buffer, 'inp', split_axis=0, concat_axis=4,...  13.2 us
    gather x2, local copies, waits for them, and re-layouts, local(): jnp.take(spectra, pick_index, axis=1)  10.8 us
    unnamed x6, local copies, waits for them, and re-layouts  10 us
    all_to_all x2, local copies, waits for them, and re-layouts, local(): lax.all_to_all(buffer, 'inp', split_axis=0, concat_axis=4, tiled=True)  9.76 us
    unnamed x1, other arithmetic  7.53 us
    dot_general x1, matrix products, local(): jnp.dot(filtered.reshape(in_dev * frame_dev, points), dft_table(), prefer...  6.4 us
  transfers between devices with their start and end apart: 2, of which 1 were waited for; matrix products, arithmetic and copies ran while one was open for 20% of the time, Pallas kernels for 0%

commit v1 on v0

v1 whole, which is shorter than its diff:
```python
import math

import jax
import jax.numpy as jnp
import numpy as np
from jax import lax
from jax.experimental import pallas as pl
from jax.experimental.pallas import tpu as pltpu
from jax.sharding import PartitionSpec as P

POINTS = 2048
HALF = POINTS // 2
CHANNELS = 768
TAPS = 4
FRAMES = 128
INPUTS = 1024
OWNERS = 128
SECS = 4
DEVS = OWNERS * SECS
IN_DEV = 8
FR_DEV = 32
ROWS = IN_DEV * FR_DEV
GROUP = FR_DEV
MIB = 1 << 20
NT = (((1,), (1,)), ((), ()))


def dft_tables():
    points = np.arange(HALF, dtype=np.int64)
    tables = []
    for parity in range(2):
        channels = np.arange(parity, CHANNELS, 2, dtype=np.int64)
        angles = (channels[:, None] * points[None, :] % POINTS) * (2.0 * math.pi / POINTS)
        tables.append(np.concatenate([np.cos(angles), -np.sin(angles)], axis=0))
    return (np.stack(tables) / math.sqrt(POINTS)).astype(jnp.bfloat16)


def pick_kernel(owner_ref, pick_ref):
    owner = owner_ref[...]

    def channel_at(axis):
        place = lax.broadcasted_iota(jnp.int32, (CHANNELS, CHANNELS), axis)
        return jnp.where(place < CHANNELS // 2, 2 * place, 2 * place - (CHANNELS - 1))

    earlier = (channel_at(0) < channel_at(1)).astype(jnp.float32).astype(jnp.bfloat16)
    owners = lax.broadcasted_iota(jnp.int32, (OWNERS, CHANNELS), 0)
    named = (owners == owner).astype(jnp.float32)
    counts = jnp.dot(named.astype(jnp.bfloat16), earlier, preferred_element_type=jnp.float32)
    rank = jnp.sum(counts * named, axis=0, keepdims=True).astype(jnp.int32)
    target = ((rank >> 1) * OWNERS + owner) * 2 + (rank & 1)
    target = jnp.where(rank < 2 * SECS, target, -1)
    for side in range(2):
        place = 2 * lax.broadcasted_iota(jnp.int32, (DEVS, CHANNELS), 0) + side
        pick_ref[side] = (place == target).astype(jnp.float32).astype(jnp.bfloat16)


def spectra_kernel(x_ref, prev_ref, w_ref, pick_ref, tab_hbm, out_ref, ext, filt, spec, picked, rows, tab, sem):
    load = pltpu.make_async_copy(tab_hbm, tab, sem)
    load.start()
    ext[:, 5:8, :] = prev_ref[...].astype(jnp.float32)
    ext[:, 8:, :] = x_ref[...].astype(jnp.float32)
    width = 256
    for chunk in range(HALF // width):
        low = pl.ds(chunk * width, width)
        high = pl.ds(HALF + chunk * width, width)

        def fir(i, lanes):
            total = jnp.zeros((FR_DEV, width), jnp.float32)
            for tap in range(TAPS):
                total = total + w_ref[tap : tap + 1, lanes] * ext[i, 8 - tap : 8 - tap + FR_DEV, lanes]
            return total

        for i in range(IN_DEV):
            first, second = fir(i, low), fir(i, high)
            filt[0, i * FR_DEV : (i + 1) * FR_DEV, low] = (first + second).astype(jnp.bfloat16)
            filt[1, i * FR_DEV : (i + 1) * FR_DEV, low] = (first - second).astype(jnp.bfloat16)
    load.wait()
    part = CHANNELS // 2
    for parity in range(2):
        both = lax.dot_general(tab[parity], filt[parity], NT, preferred_element_type=jnp.float32)
        spec[0, parity * part : (parity + 1) * part, :] = both[:part].astype(jnp.bfloat16)
        spec[1, parity * part : (parity + 1) * part, :] = both[part:].astype(jnp.bfloat16)
    here = lax.axis_index("sec")
    for place in range(4):
        kind = (place - here) & 3
        picked[place] = jnp.dot(pick_ref[kind >> 1], spec[kind & 1], preferred_element_type=jnp.float32)
    step = 64
    group = lax.broadcasted_iota(jnp.int32, (step, 128), 1) // GROUP
    lower, even = group < 2, (group & 1) == 0
    for start in range(0, DEVS, step):
        for high in range(2):
            a = [picked[k, start : start + step, high * 128 : (high + 1) * 128] for k in range(4)]
            b0 = jnp.where(lower, a[0], pltpu.roll(a[2], 64, 1))
            b2 = jnp.where(lower, pltpu.roll(a[0], 64, 1), a[2])
            b1 = jnp.where(lower, a[1], pltpu.roll(a[3], 64, 1))
            b3 = jnp.where(lower, pltpu.roll(a[1], 64, 1), a[3])
            c = [
                jnp.where(even, b0, pltpu.roll(b1, 32, 1)),
                jnp.where(even, pltpu.roll(b0, 96, 1), b1),
                jnp.where(even, b2, pltpu.roll(b3, 32, 1)),
                jnp.where(even, pltpu.roll(b2, 96, 1), b3),
            ]
            for j in range(4):
                rows[pl.ds(start * IN_DEV + high * 4 + j, step, stride=IN_DEV), :] = c[j]
        span = slice(start * IN_DEV, (start + step) * IN_DEV)
        out_ref[span, :] = rows[span, :].astype(jnp.bfloat16)


def cross_kernel(r_ref, vis_hbm, auto_ref, plain, twist, out, sems):
    step = 128
    group = lax.broadcasted_iota(jnp.int32, (step, 128), 1) // GROUP
    tile = 256
    tiles = INPUTS // tile
    above = lax.broadcasted_iota(jnp.int32, (tile, tile), 0) <= lax.broadcasted_iota(jnp.int32, (tile, tile), 1)
    on_diag = lax.broadcasted_iota(jnp.int32, (tile, tile), 0) == lax.broadcasted_iota(jnp.int32, (tile, tile), 1)
    copies = []
    for slot in range(2):
        for start in range(0, INPUTS, step):
            span = slice(start, start + step)
            got = [r_ref[x, span, :].astype(jnp.float32) for x in range(SECS)]

            def part(kind):
                value = got[(0 - kind) % 4]
                for j in range(1, 4):
                    value = jnp.where(group == j, got[(j - kind) % 4], value)
                return value

            re = part(2 * slot)
            im = pltpu.roll(part(2 * slot + 1), 96, 1)
            plain[slot, span, :128] = re.astype(jnp.bfloat16)
            plain[slot, span, 128:] = im.astype(jnp.bfloat16)
            twist[slot, span, :128] = im.astype(jnp.bfloat16)
            twist[slot, span, 128:] = (-re).astype(jnp.bfloat16)
        for r in range(tiles):
            mine = slice(r * tile, (r + 1) * tile)
            for c in range(tiles):
                other = slice(c * tile, (c + 1) * tile)
                if c >= r:
                    real = lax.dot_general(
                        plain[slot, mine, :], plain[slot, other, :], NT, preferred_element_type=jnp.float32
                    ) * (1.0 / FRAMES)
                if c <= r:
                    imag = lax.dot_general(
                        twist[slot, mine, :], plain[slot, other, :], NT, preferred_element_type=jnp.float32
                    ) * (1.0 / FRAMES)
                if c == r:
                    value = jnp.where(above, real, imag)
                    auto_ref[slot : slot + 1, other] = jnp.sum(
                        jnp.where(on_diag, real, 0.0), axis=0, keepdims=True
                    )
                else:
                    value = real if c > r else imag
                out[slot, mine, other] = value.astype(jnp.bfloat16)
            copy = pltpu.make_async_copy(out.at[slot, mine], vis_hbm.at[slot, mine], sems.at[slot, r])
            copy.start()
            copies.append(copy)
    for copy in copies:
        copy.wait()


VMEM = pl.BlockSpec(memory_space=pltpu.VMEM)
ANY = pl.BlockSpec(memory_space=pl.ANY)


def local(samples, fir_weights, channel_owner):
    last_frames = samples[:, FR_DEV - (TAPS - 1) :, :]
    previous = lax.ppermute(last_frames, "sec", [(i, i + 1) for i in range(SECS - 1)])
    owner = channel_owner.reshape(CHANNELS // 2, 2).T.reshape(1, CHANNELS)
    pick = pl.pallas_call(
        pick_kernel,
        out_shape=jax.ShapeDtypeStruct((2, DEVS, CHANNELS), jnp.bfloat16),
        in_specs=[VMEM],
        out_specs=VMEM,
        compiler_params=pltpu.CompilerParams(vmem_limit_bytes=24 * MIB),
        cost_estimate=pl.CostEstimate(flops=2 * OWNERS * CHANNELS**2, bytes_accessed=4 * MIB, transcendentals=0),
        name="pick",
    )(owner)
    buffer = pl.pallas_call(
        spectra_kernel,
        out_shape=jax.ShapeDtypeStruct((DEVS * IN_DEV, 128), jnp.bfloat16),
        in_specs=[VMEM, VMEM, VMEM, VMEM, ANY],
        out_specs=VMEM,
        scratch_shapes=[
            pltpu.VMEM((IN_DEV, 8 + FR_DEV, POINTS), jnp.float32),
            pltpu.VMEM((2, ROWS, HALF), jnp.bfloat16),
            pltpu.VMEM((2, CHANNELS, ROWS), jnp.bfloat16),
            pltpu.VMEM((4, DEVS, ROWS), jnp.float32),
            pltpu.VMEM((DEVS * IN_DEV, 128), jnp.float32),
            pltpu.VMEM((2, CHANNELS, HALF), jnp.bfloat16),
            pltpu.SemaphoreType.DMA(()),
        ],
        compiler_params=pltpu.CompilerParams(vmem_limit_bytes=32 * MIB),
        cost_estimate=pl.CostEstimate(flops=4 * ROWS * HALF * CHANNELS, bytes_accessed=8 * MIB, transcendentals=0),
        name="spectra",
    )(samples, previous, fir_weights, pick, jnp.asarray(dft_tables()))
    received = lax.all_to_all(buffer, ("sec", "inp"), split_axis=0, concat_axis=0, tiled=True)
    visibility, auto_power = pl.pallas_call(
        cross_kernel,
        out_shape=(
            jax.ShapeDtypeStruct((2, INPUTS, INPUTS), jnp.bfloat16),
            jax.ShapeDtypeStruct((2, INPUTS), jnp.float32),
        ),
        in_specs=[VMEM],
        out_specs=(ANY, VMEM),
        scratch_shapes=[
            pltpu.VMEM((2, INPUTS, 256), jnp.bfloat16),
            pltpu.VMEM((2, INPUTS, 256), jnp.bfloat16),
            pltpu.VMEM((2, INPUTS, INPUTS), jnp.bfloat16),
            pltpu.SemaphoreType.DMA((2, 4)),
        ],
        compiler_params=pltpu.CompilerParams(vmem_limit_bytes=24 * MIB),
        name="cross",
    )(received.reshape(SECS, INPUTS, 128))
    return (visibility, auto_power)


def solution(mesh):
    in_specs = (P("inp", "sec", None), P(), P())
    out_specs = (P(("inp", "sec"), None, None), P(("inp", "sec"), None))
    return jax.shard_map(local, mesh=mesh, in_specs=in_specs, out_specs=out_specs, check_vma=False)
```

time: 154 us -> 75.1 us (0.49)
  other arithmetic: 39 us -> 0 us
  local copies, waits for them, and re-layouts: 32.4 us -> 5.84 us
  waiting for transfers between devices: 13.2 us -> 0.08 us
  matrix products: 11.5 us -> 0 us
  Pallas kernels: 0 us -> 8.71 us
  blocking collectives: 48.1 us -> 55.5 us
  starting transfers between devices: 7.68 us -> 3.95 us
    neg x1 -> x0, other arithmetic: 26.2 us -> none  [dft_table(): -jnp.sin(angles)]
    all_to_all x1 -> x0, waiting for transfers between devices: 13.2 us -> none  [local(): lax.all_to_all(lax.all_to_all(buffer, 'inp', split_axis=0, concat_axis=4,...]
    dot_general x3 -> x0, matrix products: 11.5 us -> none  [the longest x1 6.4 us: local(): jnp.dot(filtered.reshape(in_dev * frame_dev, points), dft_table(), prefer...]
    gather x2 -> x0, local copies, waits for them, and re-layouts: 10.8 us -> none  [local(): jnp.take(spectra, pick_index, axis=1)]
    all_to_all x3 -> x0, local copies, waits for them, and re-layouts: 9.85 us -> none  [the longest x2 9.76 us: local(): lax.all_to_all(buffer, 'inp', split_axis=0, concat_axis=4, tiled=True)]
    pallas_call x0 -> x3, Pallas kernels: none -> 8.71 us  [the longest x1 4.25 us: local(): pl.pallas_call(spectra_kernel, out_shape=jax.ShapeDtypeStruct((DEVS * IN_...]
    unnamed x1 -> x0, other arithmetic: 7.53 us -> none
    all_to_all x1, blocking collectives: 48.1 us -> 55.5 us  [local(): lax.all_to_all(buffer, ('sec', 'inp'), split_axis=0, concat_axis=0, tiled...]
  transfers between devices with their start and end apart: 2 -> 1, of which waited for: 1 -> 1; matrix products, arithmetic and copies ran while one was open for 20% -> 1% of each run, Pallas kernels for 0% -> 1%
where the time goes in v1:
time: 75.1 us; the launch traced here: 74.8 us
  blocking collectives  55.5 us (74%)
  Pallas kernels  8.71 us (12%)
  local copies, waits for them, and re-layouts  5.84 us (8%)
  starting transfers between devices  3.95 us (5%)
    all_to_all x1, blocking collectives, local(): lax.all_to_all(buffer, ('sec', 'inp'), split_axis=0, concat_axis=0, tiled...  55.5 us
    pallas_call x1, Pallas kernels, local(): pl.pallas_call(spectra_kernel, out_shape=jax.ShapeDtypeStruct((DEVS * IN_...  4.25 us
    ppermute x1, starting transfers between devices, local(): lax.ppermute(last_frames, 'sec', [(i, i + 1) for i in range(SECS - 1)])  3.95 us
    unnamed x7, local copies, waits for them, and re-layouts  3.88 us
    pallas_call x1, Pallas kernels, local(): pl.pallas_call(cross_kernel, out_shape=(jax.ShapeDtypeStruct((2, INPUTS,...  3.58 us
  transfers between devices with their start and end apart: 1, of which 1 were waited for; matrix products, arithmetic and copies ran while one was open for 1% of the time, Pallas kernels for 1%

profile of v1, /device:TPU:1, one launch (start us, length us, event | category | flops | bytes accessed | tf_op | source)
XLA Modules:
  0.0 74.8 jit_solution(2204300030070463764)
XLA Ops:
  0.6 1.0 %slice.3 = bf16[8,3,2048]{2,1,0:T(4,128)(2,1)S(1)} slice(bf16[8,32,2048]{2,1,0:T(8,128)(2,1)} %x_ref.1), slice={[0:8], [29:32], [0:2048]} | slice | bytes 196608 | tf_op jit(solution)/shard_map/slice | solution.py:166
  1.7 4.0 %collective-permute-start = (bf16[8,3,2048]{2,1,0:T(4,128)(2,1)S(1)}, bf16[8,3,2048]{2,1,0:T(4,128)(2,1)S(1)}, u32[]{:S(2)}, u32[]{:S(2)}) collective-permute-start(bf16[8,3,2048]{2,1,0:T(4,128)(2,1)S(1)} %slice.3), channel_id=1, source_target_pairs={{0,1},{1,2},{2,3},{4,5},{5,6},{6,7},{8,9},{9,10},{10,11},{12,13},{... | collective-permute-start | bytes 294920 | tf_op jit(solution)/shard_map/ppermute | solution.py:167
  5.6 0.9 %reshape.16 = s32[384,2]{1,0:T(8,128)S(1)} reshape(s32[768]{0:T(1024)} %param.6) | data formatting | bytes 6144 | tf_op jit(solution)/shard_map/reshape | solution.py:168
  6.5 0.1 copy.6
  6.6 0.9 %pick.1.pick_ref = bf16[2,512,768]{2,1,0:T(8,128)(2,1)S(1)} custom-call(s32[1,768]{1,0:T(1,128)S(1)} %bitcast.8), custom_call_target="tpu_custom_call" | custom-call | flops 150994944 | bytes 4194304 | tf_op jit(solution)/shard_map/pick/pallas_call | solution.py:169
  7.5 0.1 collective-permute-done.prev_ref
  7.5 0.0 copy-start
  7.5 1.9 %copy-done = bf16[2,768,1024]{2,1,0:T(8,128)(2,1)S(1)} copy-done((bf16[2,768,1024]{2,1,0:T(8,128)(2,1)S(1)}, bf16[2,768,1024]{2,1,0:T(8,128)(2,1)}, u32[]{:S(2)}) %copy-start) | copy-done | bytes 3145752
  9.4 0.0 copy-start.1
  9.4 1.2 %copy-done.1 = bf16[8,32,2048]{2,1,0:T(8,128)(2,1)S(1)} copy-done((bf16[8,32,2048]{2,1,0:T(8,128)(2,1)S(1)}, bf16[8,32,2048]{2,1,0:T(8,128)(2,1)}, u32[]{:S(2)}) %copy-start.1) | copy-done | bytes 1048600
  10.7 0.0 copy-start.2
  10.7 0.8 %copy-done.2 = f32[4,2048]{1,0:T(4,128)S(1)} copy-done((f32[4,2048]{1,0:T(4,128)S(1)}, f32[4,2048]{1,0:T(4,128)}, u32[]{:S(2)}) %copy-start.2) | copy-done | bytes 32792
  11.4 4.2 %spectra.1 = bf16[4096,128]{1,0:T(8,128)(2,1)S(1)} custom-call(bf16[8,32,2048]{2,1,0:T(8,128)(2,1)S(1)} %copy-done.1, bf16[8,3,2048]{2,1,0:T(4,128)(2,1)S(1)} %collective-permute-done.prev_ref, f32[4,2048]{1,0:T(4,128)S(1)} %copy-done.2, bf16[2,512,768]{2,1,0:T(8,128)(2,1)S(1)} %pick.1.pick_ref, bf16[2,768,1024]{2,1,0:T(8,128)(2,1)S(1)} %copy-done), custom_call_target="tpu_custom_call" | custom-call | flops 805306368 | bytes 8388608 | tf_op jit(solution)/shard_map/spectra/pallas_call | solution.py:178
  15.7 55.5 %all_to_all.9 = bf16[512,8,128]{2,1,0:T(8,128)(2,1)S(1)} all-to-all(bf16[512,8,128]{2,1,0:T(8,128)(2,1)S(1)} %bitcast.7), channel_id=1, replica_groups=mesh['inp'=128,'sec'=4] {'sec','inp'}, dimensions={0} | all-to-all | bytes 2097152 | tf_op jit(solution)/shard_map/all_to_all | solution.py:196
  71.2 3.6 %cross.1 = (bf16[2,1024,1024]{2,1,0:T(8,128)(2,1)}, f32[2,1024]{1,0:T(2,128)}) custom-call(bf16[4,1024,128]{2,1,0:T(8,128)(2,1)S(1)} %bitcast.6), custom_call_target="tpu_custom_call" | custom-call | tf_op jit(solution)/shard_map/cross/pallas_call | solution.py:197
  (1 shorter events, 0.0 us)
Async XLA Ops:
  1.7 5.9 %collective-permute-start = (bf16[8,3,2048]{2,1,0:T(4,128)(2,1)S(1)}, bf16[8,3,2048]{2,1,0:T(4,128)(2,1)S(1)}, u32[]{:S(2)}, u32[]{:S(2)}) collective-permute-start(bf16[8,3,2048]{2,1,0:T(4,128)(2,1)S(1)} %slice.3), channel_id=1, source_target_pairs={{0,1},{1,2},{2,3},{4,5},{5,6},{6,7},{8,9},{9,10},{10,11},{12,13},{... | collective-permute-start | bytes 294920 | tf_op jit(solution)/shard_map/ppermute | solution.py:167
  7.5 1.9 %copy-start = (bf16[2,768,1024]{2,1,0:T(8,128)(2,1)S(1)}, bf16[2,768,1024]{2,1,0:T(8,128)(2,1)}, u32[]{:S(2)}) copy-start(bf16[2,768,1024]{2,1,0:T(8,128)(2,1)} %constant.2.clone.tab_hbm) | copy-start | bytes 9437188
  9.4 1.2 %copy-start.1 = (bf16[8,32,2048]{2,1,0:T(8,128)(2,1)S(1)}, bf16[8,32,2048]{2,1,0:T(8,128)(2,1)}, u32[]{:S(2)}) copy-start(bf16[8,32,2048]{2,1,0:T(8,128)(2,1)} %x_ref.1) | copy-start | bytes 3145732
  10.7 0.8 %copy-start.2 = (f32[4,2048]{1,0:T(4,128)S(1)}, f32[4,2048]{1,0:T(4,128)}, u32[]{:S(2)}) copy-start(f32[4,2048]{1,0:T(4,128)} %w_ref.1) | copy-start | bytes 98308

commit v2 on v1

v2 whole, which is shorter than its diff:
```python
import math

import jax
import jax.numpy as jnp
import numpy as np
from jax import lax
from jax.experimental import pallas as pl
from jax.experimental.pallas import tpu as pltpu
from jax.sharding import PartitionSpec as P

POINTS = 2048
HALF = POINTS // 2
CHANNELS = 768
PART = CHANNELS // 2
TAPS = 4
FRAMES = 128
INPUTS = 1024
OWNERS = 128
SECS = 4
DEVS = OWNERS * SECS
IN_DEV = 8
FR_DEV = 32
ROWS = IN_DEV * FR_DEV
EDGE = 8
WIDTH = 256
MIB = 1 << 20
NT = (((1,), (1,)), ((), ()))


def dft_tables():
    points = np.arange(HALF, dtype=np.int64)
    tables = []
    for parity in range(2):
        channels = np.arange(parity, CHANNELS, 2, dtype=np.int64)
        angles = (points[:, None] * channels[None, :] % POINTS) * (2.0 * math.pi / POINTS)
        tables.append(np.concatenate([np.cos(angles), -np.sin(angles)], axis=1))
    return (np.stack(tables) / math.sqrt(POINTS)).astype(jnp.bfloat16)


def as_bf16(mask):
    return mask.astype(jnp.float32).astype(jnp.bfloat16)


def pick_matrix(owner, pick_ref):
    def channel_at(axis):
        place = lax.broadcasted_iota(jnp.int32, (CHANNELS, CHANNELS), axis)
        return jnp.where(place < PART, 2 * place, 2 * place - (CHANNELS - 1))

    to_place = as_bf16(lax.broadcasted_iota(jnp.int32, (CHANNELS, CHANNELS), 0) == channel_at(1))
    spread = jnp.broadcast_to(owner.astype(jnp.float32), (8, CHANNELS)).astype(jnp.bfloat16)
    owner = jnp.dot(spread, to_place, preferred_element_type=jnp.float32)[:1].astype(jnp.int32)
    earlier = as_bf16(channel_at(0) < channel_at(1))
    named = (lax.broadcasted_iota(jnp.int32, (OWNERS, CHANNELS), 0) == owner).astype(jnp.float32)
    counts = jnp.dot(named.astype(jnp.bfloat16), earlier, preferred_element_type=jnp.float32)
    rank = jnp.sum(counts * named, axis=0, keepdims=True).astype(jnp.int32)
    target = ((rank >> 1) * OWNERS + owner) * 2 + (rank & 1)
    target = jnp.where(rank < 2 * SECS, target, -1)
    for side in range(2):
        place = 2 * lax.broadcasted_iota(jnp.int32, (DEVS, CHANNELS), 0) + side
        pick_ref[side] = as_bf16(place == target)


def head_kernel(owner_hbm, x_hbm, w_hbm, tab_hbm, pick_ref, filt_ref, edge_ref, tab_ref, owner, x, w, ext, sems):
    loads = [
        pltpu.make_async_copy(source, target, sems.at[i])
        for i, (source, target) in enumerate(((owner_hbm, owner), (x_hbm, x), (w_hbm, w), (tab_hbm, tab_ref)))
    ]
    for load in loads:
        load.start()
    loads[0].wait()
    pick_matrix(owner[...].reshape(1, CHANNELS), pick_ref)
    loads[1].wait()
    loads[2].wait()
    ext[:, :EDGE, :] = jnp.zeros((IN_DEV, EDGE, POINTS), jnp.float32)
    ext[:, EDGE:, :] = x[...].astype(jnp.float32)
    for chunk in range(HALF // WIDTH):
        low = pl.ds(chunk * WIDTH, WIDTH)
        high = pl.ds(HALF + chunk * WIDTH, WIDTH)

        def fir(i, lanes):
            total = w[0:1, lanes] * ext[i, EDGE : EDGE + FR_DEV, lanes]
            for tap in range(1, TAPS):
                total = total + w[tap : tap + 1, lanes] * ext[i, EDGE - tap : EDGE - tap + FR_DEV, lanes]
            return total

        for i in range(IN_DEV):
            first, second = fir(i, low), fir(i, high)
            edge_ref[i, :, low] = first[:EDGE]
            edge_ref[i, :, high] = second[:EDGE]
            filt_ref[0, i * FR_DEV : (i + 1) * FR_DEV, low] = (first + second).astype(jnp.bfloat16)
            filt_ref[1, i * FR_DEV : (i + 1) * FR_DEV, low] = (first - second).astype(jnp.bfloat16)
    loads[3].wait()


def spectra_kernel(prev_ref, w_ref, pick_ref, filt_ref, edge_ref, tab_ref, out_ref, ext, filt, spec, picked, rows):
    filt[...] = filt_ref[...]
    ext[:, :EDGE, :] = jnp.zeros((IN_DEV, EDGE, POINTS), jnp.float32)
    ext[:, EDGE:, :] = jnp.zeros((IN_DEV, EDGE, POINTS), jnp.float32)
    ext[:, EDGE - (TAPS - 1) : EDGE, :] = prev_ref[...].astype(jnp.float32)

    def fir(i, lanes):
        total = edge_ref[i, :, lanes]
        for tap in range(1, TAPS):
            total = total + w_ref[tap : tap + 1, lanes] * ext[i, EDGE - tap : 2 * EDGE - tap, lanes]
        return total

    for i in range(IN_DEV):
        first, second = fir(i, slice(0, HALF)), fir(i, slice(HALF, POINTS))
        filt[0, i * FR_DEV : i * FR_DEV + EDGE, :] = (first + second).astype(jnp.bfloat16)
        filt[1, i * FR_DEV : i * FR_DEV + EDGE, :] = (first - second).astype(jnp.bfloat16)
    for parity in range(2):
        both = jnp.dot(filt[parity], tab_ref[parity], preferred_element_type=jnp.float32).astype(jnp.bfloat16)
        columns = slice(parity * PART, (parity + 1) * PART)
        for i in range(IN_DEV):
            mine = both[i * FR_DEV : (i + 1) * FR_DEV]
            spec[2 * i * FR_DEV : (2 * i + 1) * FR_DEV, columns] = mine[:, :PART]
            spec[(2 * i + 1) * FR_DEV : (2 * i + 2) * FR_DEV, columns] = mine[:, PART:]
    flip = lax.axis_index("sec") & 1
    step = 64
    lower = lax.broadcasted_iota(jnp.int32, (step, 128), 1) < 64
    for quad in range(2):
        source = spec[quad * 256 : (quad + 1) * 256, :]
        for side in range(2):
            picked[quad, side] = lax.dot_general(pick_ref[side ^ flip], source, NT, preferred_element_type=jnp.float32)
        for start in range(0, DEVS, step):
            for pair in range(2):
                a, b = (picked[quad, side, start : start + step, pair * 128 : (pair + 1) * 128] for side in range(2))
                c = (jnp.where(lower, a, pltpu.roll(b, 64, 1)), jnp.where(lower, pltpu.roll(a, 64, 1), b))
                for j in range(2):
                    rows[pl.ds(start * IN_DEV + quad * 4 + pair * 2 + j, step, stride=IN_DEV), :] = c[j]
    out_ref[...] = rows[...].astype(jnp.bfloat16)


def cross_kernel(r_ref, vis_hbm, auto_ref, plain, twist, out, sems):
    tile = 256
    tiles = INPUTS // tile
    row = lax.broadcasted_iota(jnp.int32, (tile, tile), 0)
    column = lax.broadcasted_iota(jnp.int32, (tile, tile), 1)
    above, on_diag = row <= column, row == column
    turn = jnp.where(column == row - FR_DEV, 1.0, 0.0) * jnp.where((row // FR_DEV) % 2 == 1, 1.0, 0.0)
    turn = turn - jnp.where(column == row + FR_DEV, 1.0, 0.0) * jnp.where((row // FR_DEV) % 2 == 0, 1.0, 0.0)
    turn = turn.astype(jnp.bfloat16)
    lower = lax.broadcasted_iota(jnp.int32, (INPUTS, 128), 1) < 64
    copies = []
    for slot in range(2):
        for pair in range(2):
            first, second = r_ref[2 * pair + slot], r_ref[2 * pair + 1 - slot]
            plain[slot, :, pair * 128 : (pair + 1) * 128] = jnp.where(lower, first, second)
        twist[slot] = jnp.dot(plain[slot], turn, preferred_element_type=jnp.float32).astype(jnp.bfloat16)
        for r in range(tiles):
            mine = slice(r * tile, (r + 1) * tile)
            for c in range(tiles):
                other = slice(c * tile, (c + 1) * tile)
                if c >= r:
                    real = lax.dot_general(
                        plain[slot, mine, :], plain[slot, other, :], NT, preferred_element_type=jnp.float32
                    ) * (1.0 / FRAMES)
                if c <= r:
                    imag = lax.dot_general(
                        twist[slot, mine, :], plain[slot, other, :], NT, preferred_element_type=jnp.float32
                    ) * (1.0 / FRAMES)
                if c == r:
                    value = jnp.where(above, real, imag)
                    auto_ref[slot : slot + 1, other] = jnp.sum(
                        jnp.where(on_diag, real, 0.0), axis=0, keepdims=True
                    )
                else:
                    value = real if c > r else imag
                out[slot, mine, other] = value.astype(jnp.bfloat16)
            copy = pltpu.make_async_copy(out.at[slot, mine], vis_hbm.at[slot, mine], sems.at[slot, r])
            copy.start()
            copies.append(copy)
    for copy in copies:
        copy.wait()


VMEM = pl.BlockSpec(memory_space=pltpu.VMEM)
HBM = pl.BlockSpec(memory_space=pltpu.HBM)


def in_hbm(value):
    return pltpu.with_memory_space_constraint(value, pltpu.HBM)


def shaped(*shape, dtype=jnp.bfloat16):
    return jax.ShapeDtypeStruct(shape, dtype)


def local(samples, fir_weights, channel_owner):
    last_frames = samples[:, FR_DEV - (TAPS - 1) :, :]
    previous = lax.ppermute(last_frames, "sec", [(i, i + 1) for i in range(SECS - 1)])
    pick, filtered, edge, table = pl.pallas_call(
        head_kernel,
        out_shape=(
            shaped(2, DEVS, CHANNELS),
            shaped(2, ROWS, HALF),
            shaped(IN_DEV, EDGE, POINTS, dtype=jnp.float32),
            shaped(2, HALF, CHANNELS),
        ),
        in_specs=[HBM] * 4,
        out_specs=(VMEM,) * 4,
        scratch_shapes=[
            pltpu.VMEM((CHANNELS,), jnp.int32),
            pltpu.VMEM((IN_DEV, FR_DEV, POINTS), jnp.bfloat16),
            pltpu.VMEM((TAPS, POINTS), jnp.float32),
            pltpu.VMEM((IN_DEV, EDGE + FR_DEV, POINTS), jnp.float32),
            pltpu.SemaphoreType.DMA((4,)),
        ],
        compiler_params=pltpu.CompilerParams(vmem_limit_bytes=24 * MIB),
        cost_estimate=pl.CostEstimate(flops=2 * OWNERS * CHANNELS**2, bytes_accessed=8 * MIB, transcendentals=0),
        name="head",
    )(*(in_hbm(value) for value in (channel_owner, samples, fir_weights, jnp.asarray(dft_tables()))))
    buffer = pl.pallas_call(
        spectra_kernel,
        out_shape=shaped(DEVS * IN_DEV, 128),
        in_specs=[VMEM] * 6,
        out_specs=VMEM,
        scratch_shapes=[
            pltpu.VMEM((IN_DEV, 2 * EDGE, POINTS), jnp.float32),
            pltpu.VMEM((2, ROWS, HALF), jnp.bfloat16),
            pltpu.VMEM((2 * ROWS, CHANNELS), jnp.bfloat16),
            pltpu.VMEM((2, 2, DEVS, 256), jnp.float32),
            pltpu.VMEM((DEVS * IN_DEV, 128), jnp.float32),
        ],
        compiler_params=pltpu.CompilerParams(vmem_limit_bytes=32 * MIB),
        cost_estimate=pl.CostEstimate(flops=4 * ROWS * HALF * CHANNELS, bytes_accessed=8 * MIB, transcendentals=0),
        name="spectra",
    )(previous, fir_weights, pick, filtered, edge, table)
    received = lax.all_to_all(buffer, ("sec", "inp"), split_axis=0, concat_axis=0, tiled=True)
    visibility, auto_power = pl.pallas_call(
        cross_kernel,
        out_shape=(shaped(2, INPUTS, INPUTS), shaped(2, INPUTS, dtype=jnp.float32)),
        in_specs=[VMEM],
        out_specs=(HBM, VMEM),
        scratch_shapes=[
            pltpu.VMEM((2, INPUTS, 256), jnp.bfloat16),
            pltpu.VMEM((2, INPUTS, 256), jnp.bfloat16),
            pltpu.VMEM((2, INPUTS, INPUTS), jnp.bfloat16),
            pltpu.SemaphoreType.DMA((2, 4)),
        ],
        compiler_params=pltpu.CompilerParams(vmem_limit_bytes=24 * MIB),
        name="cross",
    )(received.reshape(SECS, INPUTS, 128))
    return (visibility, auto_power)


def solution(mesh):
    in_specs = (P("inp", "sec", None), P(), P())
    out_specs = (P(("inp", "sec"), None, None), P(("inp", "sec"), None))
    return jax.shard_map(local, mesh=mesh, in_specs=in_specs, out_specs=out_specs, check_vma=False)
```

time: 75.1 us -> 69.1 us (0.920)
  local copies, waits for them, and re-layouts: 5.84 us -> 1.03 us
  blocking collectives: 55.5 us -> 54.4 us
    unnamed x7 -> x2, local copies, waits for them, and re-layouts: 3.88 us -> 0.01 us
    all_to_all x1, blocking collectives: 55.5 us -> 54.4 us  [local(): lax.all_to_all(buffer, ('sec', 'inp'), split_axis=0, concat_axis=0, tiled...]
    reshape x1 -> x0, local copies, waits for them, and re-layouts: 0.85 us -> none  [local(): owner = channel_owner.reshape(CHANNELS // 2, 2).T.reshape(1, CHANNELS)]
  transfers between devices with their start and end apart: 1 -> 1, of which waited for: 1 -> 0; matrix products, arithmetic and copies ran while one was open for 1% -> 0% of each run, Pallas kernels for 1% -> 4%
where the time goes in v2:
time: 69.1 us; the launch traced here: 68.9 us
  blocking collectives  54.4 us (79%)
  Pallas kernels  8.85 us (13%)
  starting transfers between devices  3.95 us (6%)
  local copies, waits for them, and re-layouts  1.03 us (1%)
    all_to_all x1, blocking collectives, local(): lax.all_to_all(buffer, ('sec', 'inp'), split_axis=0, concat_axis=0, tiled...  54.4 us
    ppermute x1, starting transfers between devices, local(): lax.ppermute(last_frames, 'sec', [(i, i + 1) for i in range(SECS - 1)])  3.95 us
    pallas_call x1, Pallas kernels, local(): pl.pallas_call(cross_kernel, out_shape=(shaped(2, INPUTS, INPUTS), shaped...  3.41 us
    pallas_call x1, Pallas kernels, local(): pl.pallas_call(head_kernel, out_shape=(shaped(2, DEVS, CHANNELS), shaped(...  3.06 us
    pallas_call x1, Pallas kernels, local(): pl.pallas_call(spectra_kernel, out_shape=shaped(DEVS * IN_DEV, 128), in_s...  2.37 us
  transfers between devices with their start and end apart: 1, of which 0 were waited for; matrix products, arithmetic and copies ran while one was open for 0% of the time, Pallas kernels for 4%

profile of v2, /device:TPU:1, one launch (start us, length us, event | category | flops | bytes accessed | tf_op | source)
XLA Modules:
  0.0 68.9 jit_solution(16736866750756185701)
XLA Ops:
  0.6 0.0 copy-start
  0.6 1.0 %slice.3 = bf16[8,3,2048]{2,1,0:T(4,128)(2,1)S(1)} slice(bf16[8,32,2048]{2,1,0:T(8,128)(2,1)} %x_hbm.1), slice={[0:8], [29:32], [0:2048]} | slice | bytes 196608 | tf_op jit(solution)/shard_map/slice | solution.py:190
  1.7 4.0 %collective-permute-start = (bf16[8,3,2048]{2,1,0:T(4,128)(2,1)S(1)}, bf16[8,3,2048]{2,1,0:T(4,128)(2,1)S(1)}, u32[]{:S(2)}, u32[]{:S(2)}) collective-permute-start(bf16[8,3,2048]{2,1,0:T(4,128)(2,1)S(1)} %slice.3), channel_id=1, source_target_pairs={{0,1},{1,2},{2,3},{4,5},{5,6},{6,7},{8,9},{9,10},{10,11},{12,13},{... | collective-permute-start | bytes 294920 | tf_op jit(solution)/shard_map/ppermute | solution.py:191
  5.6 3.1 %head.1 = (bf16[2,512,768]{2,1,0:T(8,128)(2,1)S(1)}, bf16[2,256,1024]{2,1,0:T(8,128)(2,1)S(1)}, f32[8,8,2048]{2,1,0:T(8,128)S(1)}, bf16[2,1024,768]{2,1,0:T(8,128)(2,1)S(1)}) custom-call(s32[768]{0:T(1024)} %owner_hbm.1, bf16[8,32,2048]{2,1,0:T(8,128)(2,1)} %x_hbm.1, f32[4,2048]{1,0:T(4,128)} %w_ref.1, bf16[2,1024,768]{2,1,0:T(8,128)(2,1)} %constant.2.clone.tab_hbm), custom_call_target="tpu_custom_call" | custom-call | flops 150994944 | bytes 8388608 | tf_op jit(solution)/shard_map/head/pallas_call | solution.py:192
  8.7 0.0 collective-permute-done.prev_ref
  8.7 0.0 copy-done
  8.7 2.4 %spectra.1 = bf16[4096,128]{1,0:T(8,128)(2,1)S(1)} custom-call(bf16[8,3,2048]{2,1,0:T(4,128)(2,1)S(1)} %collective-permute-done.prev_ref, f32[4,2048]{1,0:T(4,128)S(1)} %copy-done, bf16[2,512,768]{2,1,0:T(8,128)(2,1)S(1)} %get-tuple-element.6.pick_ref, bf16[2,256,1024]{2,1,0:T(8,128)(2,1)S(1)} %get-tuple-element.7.filt_ref, ...), custom_call_target="tpu_custom_call" | custom-call | flops 805306368 | bytes 8388608 | tf_op jit(solution)/shard_map/spectra/pallas_call | solution.py:213
  11.1 54.4 %all_to_all.9 = bf16[512,8,128]{2,1,0:T(8,128)(2,1)S(1)} all-to-all(bf16[512,8,128]{2,1,0:T(8,128)(2,1)S(1)} %bitcast.2), channel_id=1, replica_groups=mesh['inp'=128,'sec'=4] {'sec','inp'}, dimensions={0} | all-to-all | bytes 2097152 | tf_op jit(solution)/shard_map/all_to_all | solution.py:229
  65.5 3.4 %cross.1 = (bf16[2,1024,1024]{2,1,0:T(8,128)(2,1)}, f32[2,1024]{1,0:T(2,128)}) custom-call(bf16[4,1024,128]{2,1,0:T(8,128)(2,1)S(1)} %bitcast.3), custom_call_target="tpu_custom_call" | custom-call | tf_op jit(solution)/shard_map/cross/pallas_call | solution.py:230
Async XLA Ops:
  0.6 8.1 %copy-start = (f32[4,2048]{1,0:T(4,128)S(1)}, f32[4,2048]{1,0:T(4,128)}, u32[]{:S(2)}) copy-start(f32[4,2048]{1,0:T(4,128)} %w_ref.1) | copy-start | bytes 98308
  1.7 7.0 %collective-permute-start = (bf16[8,3,2048]{2,1,0:T(4,128)(2,1)S(1)}, bf16[8,3,2048]{2,1,0:T(4,128)(2,1)S(1)}, u32[]{:S(2)}, u32[]{:S(2)}) collective-permute-start(bf16[8,3,2048]{2,1,0:T(4,128)(2,1)S(1)} %slice.3), channel_id=1, source_target_pairs={{0,1},{1,2},{2,3},{4,5},{5,6},{6,7},{8,9},{9,10},{10,11},{12,13},{... | collective-permute-start | bytes 294920 | tf_op jit(solution)/shard_map/ppermute | solution.py:191

commit v3 on v2

v3 whole, which is shorter than its diff:
```python
import math

import jax
import jax.numpy as jnp
import numpy as np
from jax import lax
from jax.experimental import pallas as pl
from jax.experimental.pallas import tpu as pltpu
from jax.sharding import PartitionSpec as P

POINTS = 2048
HALF = POINTS // 2
CHANNELS = 768
PART = CHANNELS // 2
TAPS = 4
FRAMES = 128
INPUTS = 1024
OWNERS = 128
SECS = 4
DEVS = OWNERS * SECS
IN_DEV = 8
FR_DEV = 32
ROWS = IN_DEV * FR_DEV
EDGE = 8
WIDTH = 256
MIB = 1 << 20
NT = (((1,), (1,)), ((), ()))


def dft_tables():
    points = np.arange(HALF, dtype=np.int64)
    tables = []
    for parity in range(2):
        channels = np.arange(parity, CHANNELS, 2, dtype=np.int64)
        angles = (points[:, None] * channels[None, :] % POINTS) * (2.0 * math.pi / POINTS)
        tables.append(np.concatenate([np.cos(angles), -np.sin(angles)], axis=1))
    return (np.stack(tables) / math.sqrt(POINTS)).astype(jnp.bfloat16)


def as_bf16(mask):
    return mask.astype(jnp.float32).astype(jnp.bfloat16)


def channel_at(axis):
    place = lax.broadcasted_iota(jnp.int32, (CHANNELS, CHANNELS), axis)
    return jnp.where(place < PART, 2 * place, 2 * place - (CHANNELS - 1))


def pick_matrix(owner, to_place, earlier, pick_ref):
    spread = jnp.broadcast_to(owner.astype(jnp.float32), (8, CHANNELS)).astype(jnp.bfloat16)
    owner = jnp.dot(spread, to_place, preferred_element_type=jnp.float32)[:1].astype(jnp.int32)
    named = (lax.broadcasted_iota(jnp.int32, (OWNERS, CHANNELS), 0) == owner).astype(jnp.float32)
    counts = jnp.dot(named.astype(jnp.bfloat16), earlier, preferred_element_type=jnp.float32)
    rank = jnp.sum(counts * named, axis=0, keepdims=True).astype(jnp.int32)
    target = ((rank >> 1) * OWNERS + owner) * 2 + (rank & 1)
    target = jnp.where(rank < 2 * SECS, target, -1)
    for side in range(2):
        place = 2 * lax.broadcasted_iota(jnp.int32, (DEVS, CHANNELS), 0) + side
        pick_ref[side] = as_bf16(place == target)


def transform(rows, frames, table, parity, spec_ref):
    both = jnp.dot(rows, table, preferred_element_type=jnp.float32).astype(jnp.bfloat16)
    columns = slice(parity * PART, (parity + 1) * PART)
    for i in range(IN_DEV):
        mine = both[i * frames : (i + 1) * frames]
        spec_ref[2 * i * FR_DEV : 2 * i * FR_DEV + frames, columns] = mine[:, :PART]
        spec_ref[(2 * i + 1) * FR_DEV : (2 * i + 1) * FR_DEV + frames, columns] = mine[:, PART:]


def head_kernel(
    owner_hbm, x_hbm, w_hbm, tab_hbm, pick_ref, spec_ref, edge_ref, tab_ref, owner, x, w, filt, to_place, earlier, sems
):
    pairs = ((owner_hbm, owner), (x_hbm, x), (w_hbm, w), (tab_hbm.at[0], tab_ref.at[0]), (tab_hbm.at[1], tab_ref.at[1]))
    loads = [pltpu.make_async_copy(source, target, sems.at[i]) for i, (source, target) in enumerate(pairs)]
    for load in loads:
        load.start()
    to_place[...] = as_bf16(lax.broadcasted_iota(jnp.int32, (CHANNELS, CHANNELS), 0) == channel_at(1))
    earlier[...] = as_bf16(channel_at(0) < channel_at(1))
    loads[0].wait()
    pick_matrix(owner[...].reshape(1, CHANNELS), to_place[...], earlier[...], pick_ref)
    loads[1].wait()
    loads[2].wait()
    frame = lax.broadcasted_iota(jnp.int32, (FR_DEV, WIDTH), 0)

    def fir(i, lanes):
        now = x[i, :, lanes].astype(jnp.float32)
        total = w[0:1, lanes] * now
        for tap in range(1, TAPS):
            total = total + w[tap : tap + 1, lanes] * jnp.where(frame >= tap, pltpu.roll(now, tap, 0), 0.0)
        return total

    for chunk in range(HALF // WIDTH):
        low = pl.ds(chunk * WIDTH, WIDTH)
        high = pl.ds(HALF + chunk * WIDTH, WIDTH)
        for i in range(IN_DEV):
            first, second = fir(i, low), fir(i, high)
            edge_ref[i, :, low] = first[:EDGE]
            edge_ref[i, :, high] = second[:EDGE]
            filt[0, i * FR_DEV : (i + 1) * FR_DEV, low] = (first + second).astype(jnp.bfloat16)
            filt[1, i * FR_DEV : (i + 1) * FR_DEV, low] = (first - second).astype(jnp.bfloat16)
    for parity in range(2):
        loads[3 + parity].wait()
        transform(filt[parity], FR_DEV, tab_ref[parity], parity, spec_ref)


def spectra_kernel(prev_ref, w_ref, pick_ref, spec_in, edge_ref, tab_ref, out_ref, spec_ref, ext, filt, picked, rows):
    spec_ref[...] = spec_in[...]
    ext[:, :EDGE, :] = jnp.zeros((IN_DEV, EDGE, POINTS), jnp.float32)
    ext[:, EDGE:, :] = jnp.zeros((IN_DEV, EDGE, POINTS), jnp.float32)
    ext[:, EDGE - (TAPS - 1) : EDGE, :] = prev_ref[...].astype(jnp.float32)

    def fir(i, lanes):
        total = edge_ref[i, :, lanes]
        for tap in range(1, TAPS):
            total = total + w_ref[tap : tap + 1, lanes] * ext[i, EDGE - tap : 2 * EDGE - tap, lanes]
        return total

    for i in range(IN_DEV):
        first, second = fir(i, slice(0, HALF)), fir(i, slice(HALF, POINTS))
        filt[0, i * EDGE : (i + 1) * EDGE, :] = (first + second).astype(jnp.bfloat16)
        filt[1, i * EDGE : (i + 1) * EDGE, :] = (first - second).astype(jnp.bfloat16)
    for parity in range(2):
        transform(filt[parity], EDGE, tab_ref[parity], parity, spec_ref)
    flip = lax.axis_index("sec") & 1
    step = 64
    lower = lax.broadcasted_iota(jnp.int32, (step, 128), 1) < 64
    for quad in range(2):
        source = spec_ref[quad * 256 : (quad + 1) * 256, :]
        for side in range(2):
            picked[quad, side] = lax.dot_general(pick_ref[side ^ flip], source, NT, preferred_element_type=jnp.float32)
        for start in range(0, DEVS, step):
            for pair in range(2):
                a, b = (picked[quad, side, start : start + step, pair * 128 : (pair + 1) * 128] for side in range(2))
                c = (jnp.where(lower, a, pltpu.roll(b, 64, 1)), jnp.where(lower, pltpu.roll(a, 64, 1), b))
                for j in range(2):
                    rows[pl.ds(start * IN_DEV + quad * 4 + pair * 2 + j, step, stride=IN_DEV), :] = c[j]
    out_ref[...] = rows[...].astype(jnp.bfloat16)


def cross_kernel(r_ref, vis_hbm, auto_hbm, plain, twist, out, auto, sems, auto_sem):
    tile, half = 256, 128
    row = lax.broadcasted_iota(jnp.int32, (tile, tile), 0)
    column = lax.broadcasted_iota(jnp.int32, (tile, tile), 1)
    odd = (row // FR_DEV) % 2
    turn = jnp.where(column - row == FR_DEV * (1 - 2 * odd), (2 * odd - 1).astype(jnp.float32), 0.0)
    turn = turn.astype(jnp.bfloat16)
    small_row = lax.broadcasted_iota(jnp.int32, (half, half), 0)
    small_column = lax.broadcasted_iota(jnp.int32, (half, half), 1)
    above, on_diag = small_row <= small_column, small_row == small_column
    lower = lax.broadcasted_iota(jnp.int32, (INPUTS, 128), 1) < 64

    def prepare(slot):
        for pair in range(2):
            first, second = r_ref[2 * pair + slot], r_ref[2 * pair + 1 - slot]
            plain[slot, :, pair * 128 : (pair + 1) * 128] = jnp.where(lower, first, second)
        twist[slot] = jnp.dot(plain[slot], turn, preferred_element_type=jnp.float32).astype(jnp.bfloat16)

    copies = []
    prepare(0)
    for slot in range(2):
        for start in range(0, INPUTS, tile):
            end = start + tile
            mine = slice(start, end)
            real = lax.dot_general(
                plain[slot, mine, :], plain[slot, start:, :], NT, preferred_element_type=jnp.float32
            ) * (1.0 / FRAMES)
            imag = lax.dot_general(
                twist[slot, mine, :], plain[slot, :end, :], NT, preferred_element_type=jnp.float32
            ) * (1.0 / FRAMES)
            if start > 0:
                out[slot, mine, :start] = imag[:, :start].astype(jnp.bfloat16)
            if end < INPUTS:
                out[slot, mine, end:] = real[:, tile:].astype(jnp.bfloat16)
            middle = start + half
            out[slot, start:middle, middle:end] = real[:half, half:tile].astype(jnp.bfloat16)
            out[slot, middle:end, start:middle] = imag[half:, start:middle].astype(jnp.bfloat16)
            for part in range(2):
                here = slice(start + part * half, start + (part + 1) * half)
                inner = slice(part * half, (part + 1) * half)
                block = real[inner, inner]
                out[slot, here, here] = jnp.where(above, block, imag[inner, here]).astype(jnp.bfloat16)
                auto[slot : slot + 1, here] = jnp.sum(jnp.where(on_diag, block, 0.0), axis=0, keepdims=True)
            copy = pltpu.make_async_copy(out.at[slot, mine], vis_hbm.at[slot, mine], sems.at[slot, start // tile])
            copy.start()
            copies.append(copy)
            if slot == 0 and start == 0:
                prepare(1)
    copy = pltpu.make_async_copy(auto, auto_hbm, auto_sem)
    copy.start()
    copies.append(copy)
    for copy in copies:
        copy.wait()


VMEM = pl.BlockSpec(memory_space=pltpu.VMEM)
HBM = pl.BlockSpec(memory_space=pltpu.HBM)


def in_hbm(value):
    return pltpu.with_memory_space_constraint(value, pltpu.HBM)


def shaped(*shape, dtype=jnp.bfloat16):
    return jax.ShapeDtypeStruct(shape, dtype)


def local(samples, fir_weights, channel_owner):
    last_frames = samples[:, FR_DEV - (TAPS - 1) :, :]
    previous = lax.ppermute(last_frames, "sec", [(i, i + 1) for i in range(SECS - 1)])
    pick, partial, edge, table = pl.pallas_call(
        head_kernel,
        out_shape=(
            shaped(2, DEVS, CHANNELS),
            shaped(2 * ROWS, CHANNELS),
            shaped(IN_DEV, EDGE, POINTS, dtype=jnp.float32),
            shaped(2, HALF, CHANNELS),
        ),
        in_specs=[HBM] * 4,
        out_specs=(VMEM,) * 4,
        scratch_shapes=[
            pltpu.VMEM((CHANNELS,), jnp.int32),
            pltpu.VMEM((IN_DEV, FR_DEV, POINTS), jnp.bfloat16),
            pltpu.VMEM((TAPS, POINTS), jnp.float32),
            pltpu.VMEM((2, ROWS, HALF), jnp.bfloat16),
            pltpu.VMEM((CHANNELS, CHANNELS), jnp.bfloat16),
            pltpu.VMEM((CHANNELS, CHANNELS), jnp.bfloat16),
            pltpu.SemaphoreType.DMA((5,)),
        ],
        compiler_params=pltpu.CompilerParams(vmem_limit_bytes=24 * MIB),
        cost_estimate=pl.CostEstimate(flops=2 * OWNERS * CHANNELS**2, bytes_accessed=8 * MIB, transcendentals=0),
        name="head",
    )(*(in_hbm(value) for value in (channel_owner, samples, fir_weights, jnp.asarray(dft_tables()))))
    buffer = pl.pallas_call(
        spectra_kernel,
        out_shape=shaped(DEVS * IN_DEV, 128),
        in_specs=[VMEM] * 6,
        out_specs=VMEM,
        scratch_shapes=[
            pltpu.VMEM((2 * ROWS, CHANNELS), jnp.bfloat16),
            pltpu.VMEM((IN_DEV, 2 * EDGE, POINTS), jnp.float32),
            pltpu.VMEM((2, IN_DEV * EDGE, HALF), jnp.bfloat16),
            pltpu.VMEM((2, 2, DEVS, 256), jnp.float32),
            pltpu.VMEM((DEVS * IN_DEV, 128), jnp.float32),
        ],
        compiler_params=pltpu.CompilerParams(vmem_limit_bytes=32 * MIB),
        cost_estimate=pl.CostEstimate(flops=4 * ROWS * HALF * CHANNELS, bytes_accessed=8 * MIB, transcendentals=0),
        name="spectra",
    )(previous, fir_weights, pick, partial, edge, table)
    received = lax.all_to_all(buffer, ("sec", "inp"), split_axis=0, concat_axis=0, tiled=True)
    visibility, auto_power = pl.pallas_call(
        cross_kernel,
        out_shape=(shaped(2, INPUTS, INPUTS), shaped(2, INPUTS, dtype=jnp.float32)),
        in_specs=[VMEM],
        out_specs=(HBM, HBM),
        scratch_shapes=[
            pltpu.VMEM((2, INPUTS, 256), jnp.bfloat16),
            pltpu.VMEM((2, INPUTS, 256), jnp.bfloat16),
            pltpu.VMEM((2, INPUTS, INPUTS), jnp.bfloat16),
            pltpu.VMEM((2, INPUTS), jnp.float32),
            pltpu.SemaphoreType.DMA((2, 4)),
            pltpu.SemaphoreType.DMA(()),
        ],
        compiler_params=pltpu.CompilerParams(vmem_limit_bytes=24 * MIB),
        name="cross",
    )(received.reshape(SECS, INPUTS, 128))
    return (visibility, auto_power)


def solution(mesh):
    in_specs = (P("inp", "sec", None), P(), P())
    out_specs = (P(("inp", "sec"), None, None), P(("inp", "sec"), None))
    return jax.shard_map(local, mesh=mesh, in_specs=in_specs, out_specs=out_specs, check_vma=False)
```

time: 69.1 us -> 68.4 us (0.990)
  blocking collectives: 54.4 us -> 53.4 us
    pallas_call x1, Pallas kernels: 3.06 us -> 4.15 us  [local(): pl.pallas_call(head_kernel, out_shape=(shaped(2, DEVS, CHANNELS), shaped(...]
    all_to_all x1, blocking collectives: 54.4 us -> 53.4 us  [local(): lax.all_to_all(buffer, ('sec', 'inp'), split_axis=0, concat_axis=0, tiled...]
  transfers between devices with their start and end apart: 1 -> 1, of which waited for: 0 -> 0; matrix products, arithmetic and copies ran while one was open for 0% -> 0% of each run, Pallas kernels for 4% -> 6%
where the time goes in v3:
time: 68.4 us; the launch traced here: 68.3 us
  blocking collectives  53.4 us (78%)
  Pallas kernels  9.15 us (13%)
  starting transfers between devices  3.95 us (6%)
  local copies, waits for them, and re-layouts  1.03 us (2%)
    all_to_all x1, blocking collectives, local(): lax.all_to_all(buffer, ('sec', 'inp'), split_axis=0, concat_axis=0, tiled...  53.4 us
    pallas_call x1, Pallas kernels, local(): pl.pallas_call(head_kernel, out_shape=(shaped(2, DEVS, CHANNELS), shaped(...  4.15 us
    ppermute x1, starting transfers between devices, local(): lax.ppermute(last_frames, 'sec', [(i, i + 1) for i in range(SECS - 1)])  3.95 us
    pallas_call x1, Pallas kernels, local(): pl.pallas_call(cross_kernel, out_shape=(shaped(2, INPUTS, INPUTS), shaped...  2.84 us
    pallas_call x1, Pallas kernels, local(): pl.pallas_call(spectra_kernel, out_shape=shaped(DEVS * IN_DEV, 128), in_s...  2.17 us
  transfers between devices with their start and end apart: 1, of which 0 were waited for; matrix products, arithmetic and copies ran while one was open for 0% of the time, Pallas kernels for 6%

profile of v3, /device:TPU:1, one launch (start us, length us, event | category | flops | bytes accessed | tf_op | source)
XLA Modules:
  0.0 68.3 jit_solution(16744781954491121454)
XLA Ops:
  0.6 0.0 copy-start
  0.6 1.0 %slice.3 = bf16[8,3,2048]{2,1,0:T(4,128)(2,1)S(1)} slice(bf16[8,32,2048]{2,1,0:T(8,128)(2,1)} %x_hbm.1), slice={[0:8], [29:32], [0:2048]} | slice | bytes 196608 | tf_op jit(solution)/shard_map/slice | solution.py:209
  1.7 4.0 %collective-permute-start = (bf16[8,3,2048]{2,1,0:T(4,128)(2,1)S(1)}, bf16[8,3,2048]{2,1,0:T(4,128)(2,1)S(1)}, u32[]{:S(2)}, u32[]{:S(2)}) collective-permute-start(bf16[8,3,2048]{2,1,0:T(4,128)(2,1)S(1)} %slice.3), channel_id=1, source_target_pairs={{0,1},{1,2},{2,3},{4,5},{5,6},{6,7},{8,9},{9,10},{10,11},{12,13},{... | collective-permute-start | bytes 294920 | tf_op jit(solution)/shard_map/ppermute | solution.py:210
  5.6 4.1 %head.1 = (bf16[2,512,768]{2,1,0:T(8,128)(2,1)S(1)}, bf16[512,768]{1,0:T(8,128)(2,1)S(1)}, f32[8,8,2048]{2,1,0:T(8,128)S(1)}, bf16[2,1024,768]{2,1,0:T(8,128)(2,1)S(1)}) custom-call(s32[768]{0:T(1024)} %owner_hbm.1, bf16[8,32,2048]{2,1,0:T(8,128)(2,1)} %x_hbm.1, f32[4,2048]{1,0:T(4,128)} %w_ref.1, bf16[2,1024,768]{2,1,0:T(8,128)(2,1)} %constant.2.clone.tab_hbm), custom_call_target="tpu_custom_call" | custom-call | flops 150994944 | bytes 8388608 | tf_op jit(solution)/shard_map/head/pallas_call | solution.py:211
  9.8 0.0 collective-permute-done.prev_ref
  9.8 0.0 copy-done
  9.8 2.2 %spectra.1 = bf16[4096,128]{1,0:T(8,128)(2,1)S(1)} custom-call(bf16[8,3,2048]{2,1,0:T(4,128)(2,1)S(1)} %collective-permute-done.prev_ref, f32[4,2048]{1,0:T(4,128)S(1)} %copy-done, bf16[2,512,768]{2,1,0:T(8,128)(2,1)S(1)} %get-tuple-element.6.pick_ref, bf16[512,768]{1,0:T(8,128)(2,1)S(1)} %get-tuple-element.7.spec_in, ...), custom_call_target="tpu_custom_call" | custom-call | flops 805306368 | bytes 8388608 | tf_op jit(solution)/shard_map/spectra/pallas_call | solution.py:234
  12.0 53.4 %all_to_all.9 = bf16[512,8,128]{2,1,0:T(8,128)(2,1)S(1)} all-to-all(bf16[512,8,128]{2,1,0:T(8,128)(2,1)S(1)} %bitcast.2), channel_id=1, replica_groups=mesh['inp'=128,'sec'=4] {'sec','inp'}, dimensions={0} | all-to-all | bytes 2097152 | tf_op jit(solution)/shard_map/all_to_all | solution.py:250
  65.4 2.8 %cross.1 = (bf16[2,1024,1024]{2,1,0:T(8,128)(2,1)}, f32[2,1024]{1,0:T(2,128)}) custom-call(bf16[4,1024,128]{2,1,0:T(8,128)(2,1)S(1)} %bitcast.3), custom_call_target="tpu_custom_call" | custom-call | tf_op jit(solution)/shard_map/cross/pallas_call | solution.py:251
Async XLA Ops:
  0.6 9.2 %copy-start = (f32[4,2048]{1,0:T(4,128)S(1)}, f32[4,2048]{1,0:T(4,128)}, u32[]{:S(2)}) copy-start(f32[4,2048]{1,0:T(4,128)} %w_ref.1) | copy-start | bytes 98308
  1.7 8.1 %collective-permute-start = (bf16[8,3,2048]{2,1,0:T(4,128)(2,1)S(1)}, bf16[8,3,2048]{2,1,0:T(4,128)(2,1)S(1)}, u32[]{:S(2)}, u32[]{:S(2)}) collective-permute-start(bf16[8,3,2048]{2,1,0:T(4,128)(2,1)S(1)} %slice.3), channel_id=1, source_target_pairs={{0,1},{1,2},{2,3},{4,5},{5,6},{6,7},{8,9},{9,10},{10,11},{12,13},{... | collective-permute-start | bytes 294920 | tf_op jit(solution)/shard_map/ppermute | solution.py:210

commit v4 on v3

--- a/solution.py
+++ b/solution.py
@@ -59,19 +59,10 @@
         pick_ref[side] = as_bf16(place == target)
 
 
-def transform(rows, frames, table, parity, spec_ref):
-    both = jnp.dot(rows, table, preferred_element_type=jnp.float32).astype(jnp.bfloat16)
-    columns = slice(parity * PART, (parity + 1) * PART)
-    for i in range(IN_DEV):
-        mine = both[i * frames : (i + 1) * frames]
-        spec_ref[2 * i * FR_DEV : 2 * i * FR_DEV + frames, columns] = mine[:, :PART]
-        spec_ref[(2 * i + 1) * FR_DEV : (2 * i + 1) * FR_DEV + frames, columns] = mine[:, PART:]
-
-
 def head_kernel(
-    owner_hbm, x_hbm, w_hbm, tab_hbm, pick_ref, spec_ref, edge_ref, tab_ref, owner, x, w, filt, to_place, earlier, sems
+    owner_hbm, x_hbm, w_hbm, tab_hbm, pick_ref, filt_ref, edge_ref, tab_ref, owner, x, w, to_place, earlier, sems
 ):
-    pairs = ((owner_hbm, owner), (x_hbm, x), (w_hbm, w), (tab_hbm.at[0], tab_ref.at[0]), (tab_hbm.at[1], tab_ref.at[1]))
+    pairs = ((owner_hbm, owner), (x_hbm, x), (w_hbm, w), (tab_hbm, tab_ref))
     loads = [pltpu.make_async_copy(source, target, sems.at[i]) for i, (source, target) in enumerate(pairs)]
     for load in loads:
         load.start()
@@ -97,15 +88,12 @@
             first, second = fir(i, low), fir(i, high)
             edge_ref[i, :, low] = first[:EDGE]
             edge_ref[i, :, high] = second[:EDGE]
-            filt[0, i * FR_DEV : (i + 1) * FR_DEV, low] = (first + second).astype(jnp.bfloat16)
-            filt[1, i * FR_DEV : (i + 1) * FR_DEV, low] = (first - second).astype(jnp.bfloat16)
-    for parity in range(2):
-        loads[3 + parity].wait()
-        transform(filt[parity], FR_DEV, tab_ref[parity], parity, spec_ref)
-
-
-def spectra_kernel(prev_ref, w_ref, pick_ref, spec_in, edge_ref, tab_ref, out_ref, spec_ref, ext, filt, picked, rows):
-    spec_ref[...] = spec_in[...]
+            filt_ref[0, i * FR_DEV : (i + 1) * FR_DEV, low] = (first + second).astype(jnp.bfloat16)
+            filt_ref[1, i * FR_DEV : (i + 1) * FR_DEV, low] = (first - second).astype(jnp.bfloat16)
+    loads[3].wait()
+
+
+def spectra_kernel(prev_ref, w_ref, pick_ref, filt_ref, edge_ref, tab_ref, out_ref, ext, filt, spec, picked, rows):
     ext[:, :EDGE, :] = jnp.zeros((IN_DEV, EDGE, POINTS), jnp.float32)
     ext[:, EDGE:, :] = jnp.zeros((IN_DEV, EDGE, POINTS), jnp.float32)
     ext[:, EDGE - (TAPS - 1) : EDGE, :] = prev_ref[...].astype(jnp.float32)
@@ -116,17 +104,23 @@
             total = total + w_ref[tap : tap + 1, lanes] * ext[i, EDGE - tap : 2 * EDGE - tap, lanes]
         return total
 
-    for i in range(IN_DEV):
-        first, second = fir(i, slice(0, HALF)), fir(i, slice(HALF, POINTS))
-        filt[0, i * EDGE : (i + 1) * EDGE, :] = (first + second).astype(jnp.bfloat16)
-        filt[1, i * EDGE : (i + 1) * EDGE, :] = (first - second).astype(jnp.bfloat16)
     for parity in range(2):
-        transform(filt[parity], EDGE, tab_ref[parity], parity, spec_ref)
+        filt[parity] = filt_ref[parity]
+        for i in range(IN_DEV):
+            first, second = fir(i, slice(0, HALF)), fir(i, slice(HALF, POINTS))
+            both = first + second if parity == 0 else first - second
+            filt[parity, i * FR_DEV : i * FR_DEV + EDGE, :] = both.astype(jnp.bfloat16)
+        both = jnp.dot(filt[parity], tab_ref[parity], preferred_element_type=jnp.float32).astype(jnp.bfloat16)
+        columns = slice(parity * PART, (parity + 1) * PART)
+        for i in range(IN_DEV):
+            mine = both[i * FR_DEV : (i + 1) * FR_DEV]
+            spec[2 * i * FR_DEV : (2 * i + 1) * FR_DEV, columns] = mine[:, :PART]
+            spec[(2 * i + 1) * FR_DEV : (2 * i + 2) * FR_DEV, columns] = mine[:, PART:]
     flip = lax.axis_index("sec") & 1
     step = 64
     lower = lax.broadcasted_iota(jnp.int32, (step, 128), 1) < 64
     for quad in range(2):
-        source = spec_ref[quad * 256 : (quad + 1) * 256, :]
+        source = spec[quad * 256 : (quad + 1) * 256, :]
         for side in range(2):
             picked[quad, side] = lax.dot_general(pick_ref[side ^ flip], source, NT, preferred_element_type=jnp.float32)
         for start in range(0, DEVS, step):
@@ -208,11 +202,11 @@
 def local(samples, fir_weights, channel_owner):
     last_frames = samples[:, FR_DEV - (TAPS - 1) :, :]
     previous = lax.ppermute(last_frames, "sec", [(i, i + 1) for i in range(SECS - 1)])
-    pick, partial, edge, table = pl.pallas_call(
+    pick, filtered, edge, table = pl.pallas_call(
         head_kernel,
         out_shape=(
             shaped(2, DEVS, CHANNELS),
-            shaped(2 * ROWS, CHANNELS),
+            shaped(2, ROWS, HALF),
             shaped(IN_DEV, EDGE, POINTS, dtype=jnp.float32),
             shaped(2, HALF, CHANNELS),
         ),
@@ -222,10 +216,9 @@
             pltpu.VMEM((CHANNELS,), jnp.int32),
             pltpu.VMEM((IN_DEV, FR_DEV, POINTS), jnp.bfloat16),
             pltpu.VMEM((TAPS, POINTS), jnp.float32),
-            pltpu.VMEM((2, ROWS, HALF), jnp.bfloat16),
             pltpu.VMEM((CHANNELS, CHANNELS), jnp.bfloat16),
             pltpu.VMEM((CHANNELS, CHANNELS), jnp.bfloat16),
-            pltpu.SemaphoreType.DMA((5,)),
+            pltpu.SemaphoreType.DMA((4,)),
         ],
         compiler_params=pltpu.CompilerParams(vmem_limit_bytes=24 * MIB),
         cost_estimate=pl.CostEstimate(flops=2 * OWNERS * CHANNELS**2, bytes_accessed=8 * MIB, transcendentals=0),
@@ -237,16 +230,16 @@
         in_specs=[VMEM] * 6,
         out_specs=VMEM,
         scratch_shapes=[
+            pltpu.VMEM((IN_DEV, 2 * EDGE, POINTS), jnp.float32),
+            pltpu.VMEM((2, ROWS, HALF), jnp.bfloat16),
             pltpu.VMEM((2 * ROWS, CHANNELS), jnp.bfloat16),
-            pltpu.VMEM((IN_DEV, 2 * EDGE, POINTS), jnp.float32),
-            pltpu.VMEM((2, IN_DEV * EDGE, HALF), jnp.bfloat16),
             pltpu.VMEM((2, 2, DEVS, 256), jnp.float32),
             pltpu.VMEM((DEVS * IN_DEV, 128), jnp.float32),
         ],
         compiler_params=pltpu.CompilerParams(vmem_limit_bytes=32 * MIB),
         cost_estimate=pl.CostEstimate(flops=4 * ROWS * HALF * CHANNELS, bytes_accessed=8 * MIB, transcendentals=0),
         name="spectra",
-    )(previous, fir_weights, pick, partial, edge, table)
+    )(previous, fir_weights, pick, filtered, edge, table)
     received = lax.all_to_all(buffer, ("sec", "inp"), split_axis=0, concat_axis=0, tiled=True)
     visibility, auto_power = pl.pallas_call(
         cross_kernel,

time: 68.4 us -> 68.6 us (level)
  blocking collectives: 53.4 us -> 54.6 us
  Pallas kernels: 9.15 us -> 8.13 us
    pallas_call x1, Pallas kernels: 4.15 us -> 2.84 us  [local(): pl.pallas_call(head_kernel, out_shape=(shaped(2, DEVS, CHANNELS), shaped(...]
    all_to_all x1, blocking collectives: 53.4 us -> 54.6 us  [local(): lax.all_to_all(buffer, ('sec', 'inp'), split_axis=0, concat_axis=0, tiled...]
  transfers between devices with their start and end apart: 1 -> 1, of which waited for: 0 -> 0; matrix products, arithmetic and copies ran while one was open for 0% -> 0% of each run, Pallas kernels for 6% -> 4%
where the time goes in v4:
time: 68.6 us; the launch traced here: 68.4 us
  blocking collectives  54.6 us (80%)
  Pallas kernels  8.13 us (12%)
  starting transfers between devices  3.95 us (6%)
  local copies, waits for them, and re-layouts  1.03 us (2%)
    all_to_all x1, blocking collectives, local(): lax.all_to_all(buffer, ('sec', 'inp'), split_axis=0, concat_axis=0, tiled...  54.6 us
    ppermute x1, starting transfers between devices, local(): lax.ppermute(last_frames, 'sec', [(i, i + 1) for i in range(SECS - 1)])  3.95 us
    pallas_call x1, Pallas kernels, local(): pl.pallas_call(cross_kernel, out_shape=(shaped(2, INPUTS, INPUTS), shaped...  2.84 us
    pallas_call x1, Pallas kernels, local(): pl.pallas_call(head_kernel, out_shape=(shaped(2, DEVS, CHANNELS), shaped(...  2.84 us
    pallas_call x1, Pallas kernels, local(): pl.pallas_call(spectra_kernel, out_shape=shaped(DEVS * IN_DEV, 128), in_s...  2.45 us
  transfers between devices with their start and end apart: 1, of which 0 were waited for; matrix products, arithmetic and copies ran while one was open for 0% of the time, Pallas kernels for 4%

profile of v4, /device:TPU:1, one launch (start us, length us, event | category | flops | bytes accessed | tf_op | source)
XLA Modules:
  0.0 68.4 jit_solution(17950326568684836926)
XLA Ops:
  0.6 0.0 copy-start
  0.6 1.0 %slice.3 = bf16[8,3,2048]{2,1,0:T(4,128)(2,1)S(1)} slice(bf16[8,32,2048]{2,1,0:T(8,128)(2,1)} %x_hbm.1), slice={[0:8], [29:32], [0:2048]} | slice | bytes 196608 | tf_op jit(solution)/shard_map/slice | solution.py:203
  1.7 4.0 %collective-permute-start = (bf16[8,3,2048]{2,1,0:T(4,128)(2,1)S(1)}, bf16[8,3,2048]{2,1,0:T(4,128)(2,1)S(1)}, u32[]{:S(2)}, u32[]{:S(2)}) collective-permute-start(bf16[8,3,2048]{2,1,0:T(4,128)(2,1)S(1)} %slice.3), channel_id=1, source_target_pairs={{0,1},{1,2},{2,3},{4,5},{5,6},{6,7},{8,9},{9,10},{10,11},{12,13},{... | collective-permute-start | bytes 294920 | tf_op jit(solution)/shard_map/ppermute | solution.py:204
  5.6 2.8 %head.1 = (bf16[2,512,768]{2,1,0:T(8,128)(2,1)S(1)}, bf16[2,256,1024]{2,1,0:T(8,128)(2,1)S(1)}, f32[8,8,2048]{2,1,0:T(8,128)S(1)}, bf16[2,1024,768]{2,1,0:T(8,128)(2,1)S(1)}) custom-call(s32[768]{0:T(1024)} %owner_hbm.1, bf16[8,32,2048]{2,1,0:T(8,128)(2,1)} %x_hbm.1, f32[4,2048]{1,0:T(4,128)} %w_ref.1, bf16[2,1024,768]{2,1,0:T(8,128)(2,1)} %constant.2.clone.tab_hbm), custom_call_target="tpu_custom_call" | custom-call | flops 150994944 | bytes 8388608 | tf_op jit(solution)/shard_map/head/pallas_call | solution.py:205
  8.5 0.0 collective-permute-done.prev_ref
  8.5 0.0 copy-done
  8.5 2.4 %spectra.1 = bf16[4096,128]{1,0:T(8,128)(2,1)S(1)} custom-call(bf16[8,3,2048]{2,1,0:T(4,128)(2,1)S(1)} %collective-permute-done.prev_ref, f32[4,2048]{1,0:T(4,128)S(1)} %copy-done, bf16[2,512,768]{2,1,0:T(8,128)(2,1)S(1)} %get-tuple-element.6.pick_ref, bf16[2,256,1024]{2,1,0:T(8,128)(2,1)S(1)} %get-tuple-element.7.filt_ref, ...), custom_call_target="tpu_custom_call" | custom-call | flops 805306368 | bytes 8388608 | tf_op jit(solution)/shard_map/spectra/pallas_call | solution.py:227
  11.0 54.6 %all_to_all.9 = bf16[512,8,128]{2,1,0:T(8,128)(2,1)S(1)} all-to-all(bf16[512,8,128]{2,1,0:T(8,128)(2,1)S(1)} %bitcast.2), channel_id=1, replica_groups=mesh['inp'=128,'sec'=4] {'sec','inp'}, dimensions={0} | all-to-all | bytes 2097152 | tf_op jit(solution)/shard_map/all_to_all | solution.py:243
  65.6 2.8 %cross.1 = (bf16[2,1024,1024]{2,1,0:T(8,128)(2,1)}, f32[2,1024]{1,0:T(2,128)}) custom-call(bf16[4,1024,128]{2,1,0:T(8,128)(2,1)S(1)} %bitcast.3), custom_call_target="tpu_custom_call" | custom-call | tf_op jit(solution)/shard_map/cross/pallas_call | solution.py:244
Async XLA Ops:
  0.6 7.9 %copy-start = (f32[4,2048]{1,0:T(4,128)S(1)}, f32[4,2048]{1,0:T(4,128)}, u32[]{:S(2)}) copy-start(f32[4,2048]{1,0:T(4,128)} %w_ref.1) | copy-start | bytes 98308
  1.7 6.8 %collective-permute-start = (bf16[8,3,2048]{2,1,0:T(4,128)(2,1)S(1)}, bf16[8,3,2048]{2,1,0:T(4,128)(2,1)S(1)}, u32[]{:S(2)}, u32[]{:S(2)}) collective-permute-start(bf16[8,3,2048]{2,1,0:T(4,128)(2,1)S(1)} %slice.3), channel_id=1, source_target_pairs={{0,1},{1,2},{2,3},{4,5},{5,6},{6,7},{8,9},{9,10},{10,11},{12,13},{... | collective-permute-start | bytes 294920 | tf_op jit(solution)/shard_map/ppermute | solution.py:204

commit v5 on v4

--- a/solution.py
+++ b/solution.py
@@ -76,10 +76,9 @@
 
     def fir(i, lanes):
         now = x[i, :, lanes].astype(jnp.float32)
-        total = w[0:1, lanes] * now
-        for tap in range(1, TAPS):
-            total = total + w[tap : tap + 1, lanes] * jnp.where(frame >= tap, pltpu.roll(now, tap, 0), 0.0)
-        return total
+        before = jnp.where(frame >= 1, pltpu.roll(now, 1, 0), 0.0)
+        older = pltpu.roll(w[2:3, lanes] * now + w[3:4, lanes] * before, 2, 0)
+        return w[0:1, lanes] * now + w[1:2, lanes] * before + jnp.where(frame >= 2, older, 0.0)
 
     for chunk in range(HALF // WIDTH):
         low = pl.ds(chunk * WIDTH, WIDTH)
@@ -129,7 +128,7 @@
                 c = (jnp.where(lower, a, pltpu.roll(b, 64, 1)), jnp.where(lower, pltpu.roll(a, 64, 1), b))
                 for j in range(2):
                     rows[pl.ds(start * IN_DEV + quad * 4 + pair * 2 + j, step, stride=IN_DEV), :] = c[j]
-    out_ref[...] = rows[...].astype(jnp.bfloat16)
+    out_ref[...] = rows[: DEVS * IN_DEV, :].astype(jnp.bfloat16)
 
 
 def cross_kernel(r_ref, vis_hbm, auto_hbm, plain, twist, out, auto, sems, auto_sem):
@@ -234,7 +233,7 @@
             pltpu.VMEM((2, ROWS, HALF), jnp.bfloat16),
             pltpu.VMEM((2 * ROWS, CHANNELS), jnp.bfloat16),
             pltpu.VMEM((2, 2, DEVS, 256), jnp.float32),
-            pltpu.VMEM((DEVS * IN_DEV, 128), jnp.float32),
+            pltpu.VMEM((DEVS * IN_DEV + 8, 128), jnp.float32),
         ],
         compiler_params=pltpu.CompilerParams(vmem_limit_bytes=32 * MIB),
         cost_estimate=pl.CostEstimate(flops=4 * ROWS * HALF * CHANNELS, bytes_accessed=8 * MIB, transcendentals=0),

time: 68.6 us -> 68.6 us (level)
  no operation moved by 1% of the time
where the time goes in v5:
time: 68.6 us; the launch traced here: 68.4 us
  blocking collectives  54.7 us (80%)
  Pallas kernels  7.98 us (12%)
  starting transfers between devices  3.95 us (6%)
  local copies, waits for them, and re-layouts  1.03 us (2%)
    all_to_all x1, blocking collectives, local(): lax.all_to_all(buffer, ('sec', 'inp'), split_axis=0, concat_axis=0, tiled...  54.7 us
    ppermute x1, starting transfers between devices, local(): lax.ppermute(last_frames, 'sec', [(i, i + 1) for i in range(SECS - 1)])  3.95 us
    pallas_call x1, Pallas kernels, local(): pl.pallas_call(cross_kernel, out_shape=(shaped(2, INPUTS, INPUTS), shaped...  2.84 us
    pallas_call x1, Pallas kernels, local(): pl.pallas_call(head_kernel, out_shape=(shaped(2, DEVS, CHANNELS), shaped(...  2.69 us
    pallas_call x1, Pallas kernels, local(): pl.pallas_call(spectra_kernel, out_shape=shaped(DEVS * IN_DEV, 128), in_s...  2.45 us
  transfers between devices with their start and end apart: 1, of which 0 were waited for; matrix products, arithmetic and copies ran while one was open for 0% of the time, Pallas kernels for 4%

profile of v5, /device:TPU:1, one launch (start us, length us, event | category | flops | bytes accessed | tf_op | source)
XLA Modules:
  0.0 68.4 jit_solution(10365113065635112987)
XLA Ops:
  0.6 0.0 copy-start
  0.6 1.0 %slice.3 = bf16[8,3,2048]{2,1,0:T(4,128)(2,1)S(1)} slice(bf16[8,32,2048]{2,1,0:T(8,128)(2,1)} %x_hbm.1), slice={[0:8], [29:32], [0:2048]} | slice | bytes 196608 | tf_op jit(solution)/shard_map/slice | solution.py:202
  1.7 4.0 %collective-permute-start = (bf16[8,3,2048]{2,1,0:T(4,128)(2,1)S(1)}, bf16[8,3,2048]{2,1,0:T(4,128)(2,1)S(1)}, u32[]{:S(2)}, u32[]{:S(2)}) collective-permute-start(bf16[8,3,2048]{2,1,0:T(4,128)(2,1)S(1)} %slice.3), channel_id=1, source_target_pairs={{0,1},{1,2},{2,3},{4,5},{5,6},{6,7},{8,9},{9,10},{10,11},{12,13},{... | collective-permute-start | bytes 294920 | tf_op jit(solution)/shard_map/ppermute | solution.py:203
  5.6 2.7 %head.1 = (bf16[2,512,768]{2,1,0:T(8,128)(2,1)S(1)}, bf16[2,256,1024]{2,1,0:T(8,128)(2,1)S(1)}, f32[8,8,2048]{2,1,0:T(8,128)S(1)}, bf16[2,1024,768]{2,1,0:T(8,128)(2,1)S(1)}) custom-call(s32[768]{0:T(1024)} %owner_hbm.1, bf16[8,32,2048]{2,1,0:T(8,128)(2,1)} %x_hbm.1, f32[4,2048]{1,0:T(4,128)} %w_ref.1, bf16[2,1024,768]{2,1,0:T(8,128)(2,1)} %constant.2.clone.tab_hbm), custom_call_target="tpu_custom_call" | custom-call | flops 150994944 | bytes 8388608 | tf_op jit(solution)/shard_map/head/pallas_call | solution.py:204
  8.3 0.0 collective-permute-done.prev_ref
  8.3 0.0 copy-done
  8.4 2.4 %spectra.1 = bf16[4096,128]{1,0:T(8,128)(2,1)S(1)} custom-call(bf16[8,3,2048]{2,1,0:T(4,128)(2,1)S(1)} %collective-permute-done.prev_ref, f32[4,2048]{1,0:T(4,128)S(1)} %copy-done, bf16[2,512,768]{2,1,0:T(8,128)(2,1)S(1)} %get-tuple-element.6.pick_ref, bf16[2,256,1024]{2,1,0:T(8,128)(2,1)S(1)} %get-tuple-element.7.filt_ref, ...), custom_call_target="tpu_custom_call" | custom-call | flops 805306368 | bytes 8388608 | tf_op jit(solution)/shard_map/spectra/pallas_call | solution.py:226
  10.8 54.7 %all_to_all.9 = bf16[512,8,128]{2,1,0:T(8,128)(2,1)S(1)} all-to-all(bf16[512,8,128]{2,1,0:T(8,128)(2,1)S(1)} %bitcast.2), channel_id=1, replica_groups=mesh['inp'=128,'sec'=4] {'sec','inp'}, dimensions={0} | all-to-all | bytes 2097152 | tf_op jit(solution)/shard_map/all_to_all | solution.py:242
  65.5 2.8 %cross.1 = (bf16[2,1024,1024]{2,1,0:T(8,128)(2,1)}, f32[2,1024]{1,0:T(2,128)}) custom-call(bf16[4,1024,128]{2,1,0:T(8,128)(2,1)S(1)} %bitcast.3), custom_call_target="tpu_custom_call" | custom-call | tf_op jit(solution)/shard_map/cross/pallas_call | solution.py:243
Async XLA Ops:
  0.6 7.7 %copy-start = (f32[4,2048]{1,0:T(4,128)S(1)}, f32[4,2048]{1,0:T(4,128)}, u32[]{:S(2)}) copy-start(f32[4,2048]{1,0:T(4,128)} %w_ref.1) | copy-start | bytes 98308
  1.7 6.7 %collective-permute-start = (bf16[8,3,2048]{2,1,0:T(4,128)(2,1)S(1)}, bf16[8,3,2048]{2,1,0:T(4,128)(2,1)S(1)}, u32[]{:S(2)}, u32[]{:S(2)}) collective-permute-start(bf16[8,3,2048]{2,1,0:T(4,128)(2,1)S(1)} %slice.3), channel_id=1, source_target_pairs={{0,1},{1,2},{2,3},{4,5},{5,6},{6,7},{8,9},{9,10},{10,11},{12,13},{... | collective-permute-start | bytes 294920 | tf_op jit(solution)/shard_map/ppermute | solution.py:203

commit v6 on v3

--- a/solution.py
+++ b/solution.py
@@ -22,6 +22,7 @@
 FR_DEV = 32
 ROWS = IN_DEV * FR_DEV
 EDGE = 8
+SPAN = FR_DEV // 2
 WIDTH = 256
 MIB = 1 << 20
 NT = (((1,), (1,)), ((), ()))
@@ -59,19 +60,31 @@
         pick_ref[side] = as_bf16(place == target)
 
 
-def transform(rows, frames, table, parity, spec_ref):
+def transform(rows, table, parity, frames, spec_refs):
     both = jnp.dot(rows, table, preferred_element_type=jnp.float32).astype(jnp.bfloat16)
     columns = slice(parity * PART, (parity + 1) * PART)
     for i in range(IN_DEV):
-        mine = both[i * frames : (i + 1) * frames]
-        spec_ref[2 * i * FR_DEV : 2 * i * FR_DEV + frames, columns] = mine[:, :PART]
-        spec_ref[(2 * i + 1) * FR_DEV : (2 * i + 1) * FR_DEV + frames, columns] = mine[:, PART:]
+        for half, spec_ref in enumerate(spec_refs):
+            size = min(frames, SPAN)
+            mine = both[i * frames + half * SPAN : i * frames + half * SPAN + size]
+            start = 2 * i * SPAN
+            spec_ref[start : start + size, columns] = mine[:, :PART]
+            spec_ref[start + SPAN : start + SPAN + size, columns] = mine[:, PART:]
+
+
+def choose(pick_ref, spec_ref, picked_ref):
+    flip = lax.axis_index("sec") & 1
+    spectra = spec_ref[...]
+    for side in range(2):
+        picked_ref[side] = lax.dot_general(pick_ref[side ^ flip], spectra, NT, preferred_element_type=jnp.float32)
 
 
 def head_kernel(
-    owner_hbm, x_hbm, w_hbm, tab_hbm, pick_ref, spec_ref, edge_ref, tab_ref, owner, x, w, filt, to_place, earlier, sems
+    owner_hbm, x_hbm, w_hbm, tab_hbm,
+    pick_ref, spec_ref, late_ref, edge_ref, tab_ref,
+    owner, x, w, filt, late_spec, to_place, earlier, sems,
 ):
-    pairs = ((owner_hbm, owner), (x_hbm, x), (w_hbm, w), (tab_hbm.at[0], tab_ref.at[0]), (tab_hbm.at[1], tab_ref.at[1]))
+    pairs = ((owner_hbm, owner), (x_hbm, x), (w_hbm, w), (tab_hbm, tab_ref))
     loads = [pltpu.make_async_copy(source, target, sems.at[i]) for i, (source, target) in enumerate(pairs)]
     for load in loads:
         load.start()
@@ -85,10 +98,9 @@
 
     def fir(i, lanes):
         now = x[i, :, lanes].astype(jnp.float32)
-        total = w[0:1, lanes] * now
-        for tap in range(1, TAPS):
-            total = total + w[tap : tap + 1, lanes] * jnp.where(frame >= tap, pltpu.roll(now, tap, 0), 0.0)
-        return total
+        before = jnp.where(frame >= 1, pltpu.roll(now, 1, 0), 0.0)
+        older = pltpu.roll(w[2:3, lanes] * now + w[3:4, lanes] * before, 2, 0)
+        return w[0:1, lanes] * now + w[1:2, lanes] * before + jnp.where(frame >= 2, older, 0.0)
 
     for chunk in range(HALF // WIDTH):
         low = pl.ds(chunk * WIDTH, WIDTH)
@@ -99,13 +111,16 @@
             edge_ref[i, :, high] = second[:EDGE]
             filt[0, i * FR_DEV : (i + 1) * FR_DEV, low] = (first + second).astype(jnp.bfloat16)
             filt[1, i * FR_DEV : (i + 1) * FR_DEV, low] = (first - second).astype(jnp.bfloat16)
+    loads[3].wait()
     for parity in range(2):
-        loads[3 + parity].wait()
-        transform(filt[parity], FR_DEV, tab_ref[parity], parity, spec_ref)
-
-
-def spectra_kernel(prev_ref, w_ref, pick_ref, spec_in, edge_ref, tab_ref, out_ref, spec_ref, ext, filt, picked, rows):
-    spec_ref[...] = spec_in[...]
+        transform(filt[parity], tab_ref[parity], parity, FR_DEV, (spec_ref, late_spec))
+    choose(pick_ref, late_spec, late_ref)
+
+
+def spectra_kernel(
+    prev_ref, w_ref, pick_ref, spec_in, late_ref, edge_ref, tab_ref, out_ref, ext, filt, spec, early, rows
+):
+    spec[...] = spec_in[...]
     ext[:, :EDGE, :] = jnp.zeros((IN_DEV, EDGE, POINTS), jnp.float32)
     ext[:, EDGE:, :] = jnp.zeros((IN_DEV, EDGE, POINTS), jnp.float32)
     ext[:, EDGE - (TAPS - 1) : EDGE, :] = prev_ref[...].astype(jnp.float32)
@@ -121,39 +136,49 @@
         filt[0, i * EDGE : (i + 1) * EDGE, :] = (first + second).astype(jnp.bfloat16)
         filt[1, i * EDGE : (i + 1) * EDGE, :] = (first - second).astype(jnp.bfloat16)
     for parity in range(2):
-        transform(filt[parity], EDGE, tab_ref[parity], parity, spec_ref)
-    flip = lax.axis_index("sec") & 1
+        transform(filt[parity], tab_ref[parity], parity, EDGE, (spec,))
+    choose(pick_ref, spec, early)
     step = 64
-    lower = lax.broadcasted_iota(jnp.int32, (step, 128), 1) < 64
-    for quad in range(2):
-        source = spec_ref[quad * 256 : (quad + 1) * 256, :]
-        for side in range(2):
-            picked[quad, side] = lax.dot_general(pick_ref[side ^ flip], source, NT, preferred_element_type=jnp.float32)
-        for start in range(0, DEVS, step):
-            for pair in range(2):
-                a, b = (picked[quad, side, start : start + step, pair * 128 : (pair + 1) * 128] for side in range(2))
-                c = (jnp.where(lower, a, pltpu.roll(b, 64, 1)), jnp.where(lower, pltpu.roll(a, 64, 1), b))
-                for j in range(2):
-                    rows[pl.ds(start * IN_DEV + quad * 4 + pair * 2 + j, step, stride=IN_DEV), :] = c[j]
-    out_ref[...] = rows[...].astype(jnp.bfloat16)
+    group = lax.broadcasted_iota(jnp.int32, (step, 128), 1) // (2 * SPAN)
+    lower, even = group < 2, (group & 1) == 0
+    for start in range(0, DEVS, step):
+        span = slice(start, start + step)
+        for quad in range(2):
+            lanes = slice(quad * 128, (quad + 1) * 128)
+            a = [source[side, span, lanes] for source in (early, late_ref) for side in range(2)]
+            b = [
+                jnp.where(lower, a[0], pltpu.roll(a[2], 64, 1)),
+                jnp.where(lower, a[1], pltpu.roll(a[3], 64, 1)),
+                jnp.where(lower, pltpu.roll(a[0], 64, 1), a[2]),
+                jnp.where(lower, pltpu.roll(a[1], 64, 1), a[3]),
+            ]
+            c = [
+                jnp.where(even, b[0], pltpu.roll(b[1], 32, 1)),
+                jnp.where(even, pltpu.roll(b[0], 96, 1), b[1]),
+                jnp.where(even, b[2], pltpu.roll(b[3], 32, 1)),
+                jnp.where(even, pltpu.roll(b[2], 96, 1), b[3]),
+            ]
+            for j in range(4):
+                rows[pl.ds(start * IN_DEV + quad * 4 + j, step, stride=IN_DEV), :] = c[j]
+    out_ref[...] = rows[: DEVS * IN_DEV, :].astype(jnp.bfloat16)
 
 
 def cross_kernel(r_ref, vis_hbm, auto_hbm, plain, twist, out, auto, sems, auto_sem):
     tile, half = 256, 128
     row = lax.broadcasted_iota(jnp.int32, (tile, tile), 0)
     column = lax.broadcasted_iota(jnp.int32, (tile, tile), 1)
-    odd = (row // FR_DEV) % 2
-    turn = jnp.where(column - row == FR_DEV * (1 - 2 * odd), (2 * odd - 1).astype(jnp.float32), 0.0)
+    odd = (row // SPAN) % 2
+    turn = jnp.where(column - row == SPAN * (1 - 2 * odd), (2 * odd - 1).astype(jnp.float32), 0.0)
     turn = turn.astype(jnp.bfloat16)
     small_row = lax.broadcasted_iota(jnp.int32, (half, half), 0)
     small_column = lax.broadcasted_iota(jnp.int32, (half, half), 1)
     above, on_diag = small_row <= small_column, small_row == small_column
-    lower = lax.broadcasted_iota(jnp.int32, (INPUTS, 128), 1) < 64
+    first_side = (lax.broadcasted_iota(jnp.int32, (INPUTS, 128), 1) // (2 * SPAN)) % 2 == 0
 
     def prepare(slot):
         for pair in range(2):
             first, second = r_ref[2 * pair + slot], r_ref[2 * pair + 1 - slot]
-            plain[slot, :, pair * 128 : (pair + 1) * 128] = jnp.where(lower, first, second)
+            plain[slot, :, pair * 128 : (pair + 1) * 128] = jnp.where(first_side, first, second)
         twist[slot] = jnp.dot(plain[slot], turn, preferred_element_type=jnp.float32).astype(jnp.bfloat16)
 
     copies = []
@@ -208,24 +233,26 @@
 def local(samples, fir_weights, channel_owner):
     last_frames = samples[:, FR_DEV - (TAPS - 1) :, :]
     previous = lax.ppermute(last_frames, "sec", [(i, i + 1) for i in range(SECS - 1)])
-    pick, partial, edge, table = pl.pallas_call(
+    pick, spectra, late, edge, table = pl.pallas_call(
         head_kernel,
         out_shape=(
             shaped(2, DEVS, CHANNELS),
-            shaped(2 * ROWS, CHANNELS),
+            shaped(ROWS, CHANNELS),
+            shaped(2, DEVS, ROWS, dtype=jnp.float32),
             shaped(IN_DEV, EDGE, POINTS, dtype=jnp.float32),
             shaped(2, HALF, CHANNELS),
         ),
         in_specs=[HBM] * 4,
-        out_specs=(VMEM,) * 4,
+        out_specs=(VMEM,) * 5,
         scratch_shapes=[
             pltpu.VMEM((CHANNELS,), jnp.int32),
             pltpu.VMEM((IN_DEV, FR_DEV, POINTS), jnp.bfloat16),
             pltpu.VMEM((TAPS, POINTS), jnp.float32),
             pltpu.VMEM((2, ROWS, HALF), jnp.bfloat16),
+            pltpu.VMEM((ROWS, CHANNELS), jnp.bfloat16),
             pltpu.VMEM((CHANNELS, CHANNELS), jnp.bfloat16),
             pltpu.VMEM((CHANNELS, CHANNELS), jnp.bfloat16),
-            pltpu.SemaphoreType.DMA((5,)),
+            pltpu.SemaphoreType.DMA((4,)),
         ],
         compiler_params=pltpu.CompilerParams(vmem_limit_bytes=24 * MIB),
         cost_estimate=pl.CostEstimate(flops=2 * OWNERS * CHANNELS**2, bytes_accessed=8 * MIB, transcendentals=0),
@@ -234,19 +261,19 @@
     buffer = pl.pallas_call(
         spectra_kernel,
         out_shape=shaped(DEVS * IN_DEV, 128),
-        in_specs=[VMEM] * 6,
+        in_specs=[VMEM] * 7,
         out_specs=VMEM,
         scratch_shapes=[
-            pltpu.VMEM((2 * ROWS, CHANNELS), jnp.bfloat16),
             pltpu.VMEM((IN_DEV, 2 * EDGE, POINTS), jnp.float32),
             pltpu.VMEM((2, IN_DEV * EDGE, HALF), jnp.bfloat16),
-            pltpu.VMEM((2, 2, DEVS, 256), jnp.float32),
-            pltpu.VMEM((DEVS * IN_DEV, 128), jnp.float32),
+            pltpu.VMEM((ROWS, CHANNELS), jnp.bfloat16),
+            pltpu.VMEM((2, DEVS, ROWS), jnp.float32),
+            pltpu.VMEM((DEVS * IN_DEV + 8, 128), jnp.float32),
         ],
         compiler_params=pltpu.CompilerParams(vmem_limit_bytes=32 * MIB),
         cost_estimate=pl.CostEstimate(flops=4 * ROWS * HALF * CHANNELS, bytes_accessed=8 * MIB, transcendentals=0),
         name="spectra",
-    )(previous, fir_weights, pick, partial, edge, table)
+    )(previous, fir_weights, pick, spectra, late, edge, table)
     received = lax.all_to_all(buffer, ("sec", "inp"), split_axis=0, concat_axis=0, tiled=True)
     visibility, auto_power = pl.pallas_call(
         cross_kernel,

time: 68.4 us -> 68.4 us (level)
  no operation moved by 1% of the time
where the time goes in v6:
time: 68.4 us; the launch traced here: 68.2 us
  blocking collectives  53.4 us (78%)
  Pallas kernels  9.1 us (13%)
  starting transfers between devices  3.95 us (6%)
  local copies, waits for them, and re-layouts  1.03 us (2%)
    all_to_all x1, blocking collectives, local(): lax.all_to_all(buffer, ('sec', 'inp'), split_axis=0, concat_axis=0, tiled...  53.4 us
    pallas_call x1, Pallas kernels, local(): pl.pallas_call(head_kernel, out_shape=(shaped(2, DEVS, CHANNELS), shaped(...  3.99 us
    ppermute x1, starting transfers between devices, local(): lax.ppermute(last_frames, 'sec', [(i, i + 1) for i in range(SECS - 1)])  3.95 us
    pallas_call x1, Pallas kernels, local(): pl.pallas_call(cross_kernel, out_shape=(shaped(2, INPUTS, INPUTS), shaped...  2.83 us
    pallas_call x1, Pallas kernels, local(): pl.pallas_call(spectra_kernel, out_shape=shaped(DEVS * IN_DEV, 128), in_s...  2.27 us
  transfers between devices with their start and end apart: 1, of which 0 were waited for; matrix products, arithmetic and copies ran while one was open for 0% of the time, Pallas kernels for 6%

profile of v6, /device:TPU:1, one launch (start us, length us, event | category | flops | bytes accessed | tf_op | source)
XLA Modules:
  0.0 68.2 jit_solution(2131008635490943405)
XLA Ops:
  0.6 0.0 copy-start
  0.6 1.0 %slice.3 = bf16[8,3,2048]{2,1,0:T(4,128)(2,1)S(1)} slice(bf16[8,32,2048]{2,1,0:T(8,128)(2,1)} %x_hbm.1), slice={[0:8], [29:32], [0:2048]} | slice | bytes 196608 | tf_op jit(solution)/shard_map/slice | solution.py:234
  1.7 4.0 %collective-permute-start = (bf16[8,3,2048]{2,1,0:T(4,128)(2,1)S(1)}, bf16[8,3,2048]{2,1,0:T(4,128)(2,1)S(1)}, u32[]{:S(2)}, u32[]{:S(2)}) collective-permute-start(bf16[8,3,2048]{2,1,0:T(4,128)(2,1)S(1)} %slice.3), channel_id=1, source_target_pairs={{0,1},{1,2},{2,3},{4,5},{5,6},{6,7},{8,9},{9,10},{10,11},{12,13},{... | collective-permute-start | bytes 294920 | tf_op jit(solution)/shard_map/ppermute | solution.py:235
  5.6 4.0 %head.1 = (bf16[2,512,768]{2,1,0:T(8,128)(2,1)S(1)}, bf16[256,768]{1,0:T(8,128)(2,1)S(1)}, f32[2,512,256]{2,1,0:T(8,128)S(1)}, f32[8,8,2048]{2,1,0:T(8,128)S(1)}, bf16[2,1024,768]{2,1,0:T(8,128)(2,1)S(1)}) custom-call(s32[768]{0:T(1024)} %owner_hbm.1, bf16[8,32,2048]{2,1,0:T(8,128)(2,1)} %x_hbm.1, f32[4,2048]{1,0:T(4,128)} %w_ref.1, ...), custom_call_target="tpu_custom_call" | custom-call | flops 150994944 | bytes 8388608 | tf_op jit(solution)/shard_map/head/pallas_call | solution.py:236
  9.6 0.0 collective-permute-done.prev_ref
  9.6 0.0 copy-done
  9.7 2.3 %spectra.1 = bf16[4096,128]{1,0:T(8,128)(2,1)S(1)} custom-call(bf16[8,3,2048]{2,1,0:T(4,128)(2,1)S(1)} %collective-permute-done.prev_ref, f32[4,2048]{1,0:T(4,128)S(1)} %copy-done, bf16[2,512,768]{2,1,0:T(8,128)(2,1)S(1)} %get-tuple-element.7.pick_ref, bf16[256,768]{1,0:T(8,128)(2,1)S(1)} %get-tuple-element.8.spec_in, ...), custom_call_target="tpu_custom_call" | custom-call | flops 805306368 | bytes 8388608 | tf_op jit(solution)/shard_map/spectra/pallas_call | solution.py:261
  11.9 53.4 %all_to_all.9 = bf16[512,8,128]{2,1,0:T(8,128)(2,1)S(1)} all-to-all(bf16[512,8,128]{2,1,0:T(8,128)(2,1)S(1)} %bitcast.2), channel_id=1, replica_groups=mesh['inp'=128,'sec'=4] {'sec','inp'}, dimensions={0} | all-to-all | bytes 2097152 | tf_op jit(solution)/shard_map/all_to_all | solution.py:277
  65.4 2.8 %cross.1 = (bf16[2,1024,1024]{2,1,0:T(8,128)(2,1)}, f32[2,1024]{1,0:T(2,128)}) custom-call(bf16[4,1024,128]{2,1,0:T(8,128)(2,1)S(1)} %bitcast.3), custom_call_target="tpu_custom_call" | custom-call | tf_op jit(solution)/shard_map/cross/pallas_call | solution.py:278
Async XLA Ops:
  0.6 9.0 %copy-start = (f32[4,2048]{1,0:T(4,128)S(1)}, f32[4,2048]{1,0:T(4,128)}, u32[]{:S(2)}) copy-start(f32[4,2048]{1,0:T(4,128)} %w_ref.1) | copy-start | bytes 98308
  1.7 8.0 %collective-permute-start = (bf16[8,3,2048]{2,1,0:T(4,128)(2,1)S(1)}, bf16[8,3,2048]{2,1,0:T(4,128)(2,1)S(1)}, u32[]{:S(2)}, u32[]{:S(2)}) collective-permute-start(bf16[8,3,2048]{2,1,0:T(4,128)(2,1)S(1)} %slice.3), channel_id=1, source_target_pairs={{0,1},{1,2},{2,3},{4,5},{5,6},{6,7},{8,9},{9,10},{10,11},{12,13},{... | collective-permute-start | bytes 294920 | tf_op jit(solution)/shard_map/ppermute | solution.py:235

commit v7 on v6

--- a/solution.py
+++ b/solution.py
@@ -63,20 +63,22 @@
 def transform(rows, table, parity, frames, spec_refs):
     both = jnp.dot(rows, table, preferred_element_type=jnp.float32).astype(jnp.bfloat16)
     columns = slice(parity * PART, (parity + 1) * PART)
+    size = min(frames, SPAN)
     for i in range(IN_DEV):
         for half, spec_ref in enumerate(spec_refs):
-            size = min(frames, SPAN)
             mine = both[i * frames + half * SPAN : i * frames + half * SPAN + size]
-            start = 2 * i * SPAN
-            spec_ref[start : start + size, columns] = mine[:, :PART]
-            spec_ref[start + SPAN : start + SPAN + size, columns] = mine[:, PART:]
+            for side in range(2):
+                start = (i // 4) * 128 + ((i + 2 * half + side) % 4) * 2 * SPAN
+                spec_ref[side, start : start + size, columns] = mine[:, :PART]
+                spec_ref[side, start + SPAN : start + SPAN + size, columns] = mine[:, PART:]
 
 
 def choose(pick_ref, spec_ref, picked_ref):
     flip = lax.axis_index("sec") & 1
-    spectra = spec_ref[...]
     for side in range(2):
-        picked_ref[side] = lax.dot_general(pick_ref[side ^ flip], spectra, NT, preferred_element_type=jnp.float32)
+        picked_ref[side] = lax.dot_general(
+            pick_ref[side ^ flip], spec_ref[side], NT, preferred_element_type=jnp.float32
+        )
 
 
 def head_kernel(
@@ -146,20 +148,14 @@
         for quad in range(2):
             lanes = slice(quad * 128, (quad + 1) * 128)
             a = [source[side, span, lanes] for source in (early, late_ref) for side in range(2)]
-            b = [
-                jnp.where(lower, a[0], pltpu.roll(a[2], 64, 1)),
-                jnp.where(lower, a[1], pltpu.roll(a[3], 64, 1)),
-                jnp.where(lower, pltpu.roll(a[0], 64, 1), a[2]),
-                jnp.where(lower, pltpu.roll(a[1], 64, 1), a[3]),
-            ]
-            c = [
-                jnp.where(even, b[0], pltpu.roll(b[1], 32, 1)),
-                jnp.where(even, pltpu.roll(b[0], 96, 1), b[1]),
-                jnp.where(even, b[2], pltpu.roll(b[3], 32, 1)),
-                jnp.where(even, pltpu.roll(b[2], 96, 1), b[3]),
-            ]
             for j in range(4):
-                rows[pl.ds(start * IN_DEV + quad * 4 + j, step, stride=IN_DEV), :] = c[j]
+                turned = [a[(place - j) % 4] for place in range(4)]
+                value = jnp.where(
+                    lower, jnp.where(even, turned[0], turned[1]), jnp.where(even, turned[2], turned[3])
+                )
+                if j > 0:
+                    value = pltpu.roll(value, 128 - 2 * SPAN * j, 1)
+                rows[pl.ds(start * IN_DEV + quad * 4 + j, step, stride=IN_DEV), :] = value
     out_ref[...] = rows[: DEVS * IN_DEV, :].astype(jnp.bfloat16)
 
 
@@ -237,7 +233,7 @@
         head_kernel,
         out_shape=(
             shaped(2, DEVS, CHANNELS),
-            shaped(ROWS, CHANNELS),
+            shaped(2, ROWS, CHANNELS),
             shaped(2, DEVS, ROWS, dtype=jnp.float32),
             shaped(IN_DEV, EDGE, POINTS, dtype=jnp.float32),
             shaped(2, HALF, CHANNELS),
@@ -249,7 +245,7 @@
             pltpu.VMEM((IN_DEV, FR_DEV, POINTS), jnp.bfloat16),
             pltpu.VMEM((TAPS, POINTS), jnp.float32),
             pltpu.VMEM((2, ROWS, HALF), jnp.bfloat16),
-            pltpu.VMEM((ROWS, CHANNELS), jnp.bfloat16),
+            pltpu.VMEM((2, ROWS, CHANNELS), jnp.bfloat16),
             pltpu.VMEM((CHANNELS, CHANNELS), jnp.bfloat16),
             pltpu.VMEM((CHANNELS, CHANNELS), jnp.bfloat16),
             pltpu.SemaphoreType.DMA((4,)),
@@ -266,7 +262,7 @@
         scratch_shapes=[
             pltpu.VMEM((IN_DEV, 2 * EDGE, POINTS), jnp.float32),
             pltpu.VMEM((2, IN_DEV * EDGE, HALF), jnp.bfloat16),
-            pltpu.VMEM((ROWS, CHANNELS), jnp.bfloat16),
+            pltpu.VMEM((2, ROWS, CHANNELS), jnp.bfloat16),
             pltpu.VMEM((2, DEVS, ROWS), jnp.float32),
             pltpu.VMEM((DEVS * IN_DEV + 8, 128), jnp.float32),
         ],

time: 68.4 us -> 68.1 us (level)
  no operation moved by 1% of the time
where the time goes in v7:
time: 68.1 us; the launch traced here: 67.9 us
  blocking collectives  53.4 us (78%)
  Pallas kernels  8.78 us (13%)
  starting transfers between devices  3.95 us (6%)
  local copies, waits for them, and re-layouts  1.03 us (2%)
    all_to_all x1, blocking collectives, local(): lax.all_to_all(buffer, ('sec', 'inp'), split_axis=0, concat_axis=0, tiled...  53.4 us
    pallas_call x1, Pallas kernels, local(): pl.pallas_call(head_kernel, out_shape=(shaped(2, DEVS, CHANNELS), shaped(...  3.99 us
    ppermute x1, starting transfers between devices, local(): lax.ppermute(last_frames, 'sec', [(i, i + 1) for i in range(SECS - 1)])  3.95 us
    pallas_call x1, Pallas kernels, local(): pl.pallas_call(cross_kernel, out_shape=(shaped(2, INPUTS, INPUTS), shaped...  2.83 us
    pallas_call x1, Pallas kernels, local(): pl.pallas_call(spectra_kernel, out_shape=shaped(DEVS * IN_DEV, 128), in_s...  1.96 us
  transfers between devices with their start and end apart: 1, of which 0 were waited for; matrix products, arithmetic and copies ran while one was open for 0% of the time, Pallas kernels for 6%

profile of v7, /device:TPU:1, one launch (start us, length us, event | category | flops | bytes accessed | tf_op | source)
XLA Modules:
  0.0 67.9 jit_solution(954826387811364209)
XLA Ops:
  0.6 0.0 copy-start
  0.6 1.0 %slice.3 = bf16[8,3,2048]{2,1,0:T(4,128)(2,1)S(1)} slice(bf16[8,32,2048]{2,1,0:T(8,128)(2,1)} %x_hbm.1), slice={[0:8], [29:32], [0:2048]} | slice | bytes 196608 | tf_op jit(solution)/shard_map/slice | solution.py:230
  1.7 4.0 %collective-permute-start = (bf16[8,3,2048]{2,1,0:T(4,128)(2,1)S(1)}, bf16[8,3,2048]{2,1,0:T(4,128)(2,1)S(1)}, u32[]{:S(2)}, u32[]{:S(2)}) collective-permute-start(bf16[8,3,2048]{2,1,0:T(4,128)(2,1)S(1)} %slice.3), channel_id=1, source_target_pairs={{0,1},{1,2},{2,3},{4,5},{5,6},{6,7},{8,9},{9,10},{10,11},{12,13},{... | collective-permute-start | bytes 294920 | tf_op jit(solution)/shard_map/ppermute | solution.py:231
  5.6 4.0 %head.1 = (bf16[2,512,768]{2,1,0:T(8,128)(2,1)S(1)}, bf16[2,256,768]{2,1,0:T(8,128)(2,1)S(1)}, f32[2,512,256]{2,1,0:T(8,128)S(1)}, f32[8,8,2048]{2,1,0:T(8,128)S(1)}, bf16[2,1024,768]{2,1,0:T(8,128)(2,1)S(1)}) custom-call(s32[768]{0:T(1024)} %owner_hbm.1, bf16[8,32,2048]{2,1,0:T(8,128)(2,1)} %x_hbm.1, f32[4,2048]{1,0:T(4,128)} %w_ref.1, ...), custom_call_target="tpu_custom_call" | custom-call | flops 150994944 | bytes 8388608 | tf_op jit(solution)/shard_map/head/pallas_call | solution.py:232
  9.6 0.0 collective-permute-done.prev_ref
  9.6 0.0 copy-done
  9.7 2.0 %spectra.1 = bf16[4096,128]{1,0:T(8,128)(2,1)S(1)} custom-call(bf16[8,3,2048]{2,1,0:T(4,128)(2,1)S(1)} %collective-permute-done.prev_ref, f32[4,2048]{1,0:T(4,128)S(1)} %copy-done, bf16[2,512,768]{2,1,0:T(8,128)(2,1)S(1)} %get-tuple-element.7.pick_ref, bf16[2,256,768]{2,1,0:T(8,128)(2,1)S(1)} %get-tuple-element.8.spec_in, ...), custom_call_target="tpu_custom_call" | custom-call | flops 805306368 | bytes 8388608 | tf_op jit(solution)/shard_map/spectra/pallas_call | solution.py:257
  11.6 53.4 %all_to_all.9 = bf16[512,8,128]{2,1,0:T(8,128)(2,1)S(1)} all-to-all(bf16[512,8,128]{2,1,0:T(8,128)(2,1)S(1)} %bitcast.3), channel_id=1, replica_groups=mesh['inp'=128,'sec'=4] {'sec','inp'}, dimensions={0} | all-to-all | bytes 2097152 | tf_op jit(solution)/shard_map/all_to_all | solution.py:273
  65.1 2.8 %cross.1 = (bf16[2,1024,1024]{2,1,0:T(8,128)(2,1)}, f32[2,1024]{1,0:T(2,128)}) custom-call(bf16[4,1024,128]{2,1,0:T(8,128)(2,1)S(1)} %bitcast.2), custom_call_target="tpu_custom_call" | custom-call | tf_op jit(solution)/shard_map/cross/pallas_call | solution.py:274
Async XLA Ops:
  0.6 9.0 %copy-start = (f32[4,2048]{1,0:T(4,128)S(1)}, f32[4,2048]{1,0:T(4,128)}, u32[]{:S(2)}) copy-start(f32[4,2048]{1,0:T(4,128)} %w_ref.1) | copy-start | bytes 98308
  1.7 8.0 %collective-permute-start = (bf16[8,3,2048]{2,1,0:T(4,128)(2,1)S(1)}, bf16[8,3,2048]{2,1,0:T(4,128)(2,1)S(1)}, u32[]{:S(2)}, u32[]{:S(2)}) collective-permute-start(bf16[8,3,2048]{2,1,0:T(4,128)(2,1)S(1)} %slice.3), channel_id=1, source_target_pairs={{0,1},{1,2},{2,3},{4,5},{5,6},{6,7},{8,9},{9,10},{10,11},{12,13},{... | collective-permute-start | bytes 294920 | tf_op jit(solution)/shard_map/ppermute | solution.py:231

commit v8 on v7

--- a/solution.py
+++ b/solution.py
@@ -22,6 +22,7 @@
 FR_DEV = 32
 ROWS = IN_DEV * FR_DEV
 EDGE = 8
+REDO = EDGE // 2
 SPAN = FR_DEV // 2
 WIDTH = 256
 MIB = 1 << 20
@@ -60,8 +61,11 @@
         pick_ref[side] = as_bf16(place == target)
 
 
-def transform(rows, table, parity, frames, spec_refs):
-    both = jnp.dot(rows, table, preferred_element_type=jnp.float32).astype(jnp.bfloat16)
+def transform(rows, table):
+    return jnp.dot(rows, table, preferred_element_type=jnp.float32).astype(jnp.bfloat16)
+
+
+def place(both, parity, frames, spec_refs):
     columns = slice(parity * PART, (parity + 1) * PART)
     size = min(frames, SPAN)
     for i in range(IN_DEV):
@@ -115,30 +119,33 @@
             filt[1, i * FR_DEV : (i + 1) * FR_DEV, low] = (first - second).astype(jnp.bfloat16)
     loads[3].wait()
     for parity in range(2):
-        transform(filt[parity], tab_ref[parity], parity, FR_DEV, (spec_ref, late_spec))
+        place(transform(filt[parity], tab_ref[parity]), parity, FR_DEV, (spec_ref, late_spec))
     choose(pick_ref, late_spec, late_ref)
 
 
 def spectra_kernel(
     prev_ref, w_ref, pick_ref, spec_in, late_ref, edge_ref, tab_ref, out_ref, ext, filt, spec, early, rows
 ):
-    spec[...] = spec_in[...]
-    ext[:, :EDGE, :] = jnp.zeros((IN_DEV, EDGE, POINTS), jnp.float32)
-    ext[:, EDGE:, :] = jnp.zeros((IN_DEV, EDGE, POINTS), jnp.float32)
-    ext[:, EDGE - (TAPS - 1) : EDGE, :] = prev_ref[...].astype(jnp.float32)
+    ext[:, EDGE - (TAPS - 1) :, :] = prev_ref[...].astype(jnp.float32)
+    frame = lax.broadcasted_iota(jnp.int32, (EDGE, HALF), 0)
 
     def fir(i, lanes):
+        halo = ext[i, :, lanes]
         total = edge_ref[i, :, lanes]
         for tap in range(1, TAPS):
-            total = total + w_ref[tap : tap + 1, lanes] * ext[i, EDGE - tap : 2 * EDGE - tap, lanes]
+            total = total + jnp.where(frame < tap, w_ref[tap : tap + 1, lanes] * pltpu.roll(halo, tap, 0), 0.0)
         return total
 
-    for i in range(IN_DEV):
-        first, second = fir(i, slice(0, HALF)), fir(i, slice(HALF, POINTS))
-        filt[0, i * EDGE : (i + 1) * EDGE, :] = (first + second).astype(jnp.bfloat16)
-        filt[1, i * EDGE : (i + 1) * EDGE, :] = (first - second).astype(jnp.bfloat16)
+    for i in range(0, IN_DEV, 2):
+        pair = [(fir(k, slice(0, HALF)), fir(k, slice(HALF, POINTS))) for k in (i, i + 1)]
+        for parity in range(2):
+            mine, other = (first + second if parity == 0 else first - second for first, second in pair)
+            both = jnp.where(frame < REDO, mine, pltpu.roll(other, REDO, 0))
+            filt[parity, i * REDO : (i + 2) * REDO, :] = both.astype(jnp.bfloat16)
+    again = [transform(filt[parity], tab_ref[parity]) for parity in range(2)]
+    spec[...] = spec_in[...]
     for parity in range(2):
-        transform(filt[parity], tab_ref[parity], parity, EDGE, (spec,))
+        place(again[parity], parity, REDO, (spec,))
     choose(pick_ref, spec, early)
     step = 64
     group = lax.broadcasted_iota(jnp.int32, (step, 128), 1) // (2 * SPAN)
@@ -260,8 +267,8 @@
         in_specs=[VMEM] * 7,
         out_specs=VMEM,
         scratch_shapes=[
-            pltpu.VMEM((IN_DEV, 2 * EDGE, POINTS), jnp.float32),
-            pltpu.VMEM((2, IN_DEV * EDGE, HALF), jnp.bfloat16),
+            pltpu.VMEM((IN_DEV, EDGE, POINTS), jnp.float32),
+            pltpu.VMEM((2, IN_DEV * REDO, HALF), jnp.bfloat16),
             pltpu.VMEM((2, ROWS, CHANNELS), jnp.bfloat16),
             pltpu.VMEM((2, DEVS, ROWS), jnp.float32),
             pltpu.VMEM((DEVS * IN_DEV + 8, 128), jnp.float32),

time: 68.1 us -> 67.9 us (level)
  no operation moved by 1% of the time
where the time goes in v8:
time: 67.9 us; the launch traced here: 67.7 us
  blocking collectives  53.4 us (79%)
  Pallas kernels  8.58 us (13%)
  starting transfers between devices  3.95 us (6%)
  local copies, waits for them, and re-layouts  1.03 us (2%)
  between operations  0.68 us (1%)
    all_to_all x1, blocking collectives, local(): lax.all_to_all(buffer, ('sec', 'inp'), split_axis=0, concat_axis=0, tiled...  53.4 us
    pallas_call x1, Pallas kernels, local(): pl.pallas_call(head_kernel, out_shape=(shaped(2, DEVS, CHANNELS), shaped(...  3.99 us
    ppermute x1, starting transfers between devices, local(): lax.ppermute(last_frames, 'sec', [(i, i + 1) for i in range(SECS - 1)])  3.95 us
    pallas_call x1, Pallas kernels, local(): pl.pallas_call(cross_kernel, out_shape=(shaped(2, INPUTS, INPUTS), shaped...  2.83 us
    pallas_call x1, Pallas kernels, local(): pl.pallas_call(spectra_kernel, out_shape=shaped(DEVS * IN_DEV, 128), in_s...  1.76 us
  transfers between devices with their start and end apart: 1, of which 0 were waited for; matrix products, arithmetic and copies ran while one was open for 0% of the time, Pallas kernels for 6%

profile of v8, /device:TPU:1, one launch (start us, length us, event | category | flops | bytes accessed | tf_op | source)
XLA Modules:
  0.0 67.7 jit_solution(8735786734890567337)
XLA Ops:
  0.6 0.0 copy-start
  0.6 1.0 %slice.3 = bf16[8,3,2048]{2,1,0:T(4,128)(2,1)S(1)} slice(bf16[8,32,2048]{2,1,0:T(8,128)(2,1)} %x_hbm.1), slice={[0:8], [29:32], [0:2048]} | slice | bytes 196608 | tf_op jit(solution)/shard_map/slice | solution.py:237
  1.7 4.0 %collective-permute-start = (bf16[8,3,2048]{2,1,0:T(4,128)(2,1)S(1)}, bf16[8,3,2048]{2,1,0:T(4,128)(2,1)S(1)}, u32[]{:S(2)}, u32[]{:S(2)}) collective-permute-start(bf16[8,3,2048]{2,1,0:T(4,128)(2,1)S(1)} %slice.3), channel_id=1, source_target_pairs={{0,1},{1,2},{2,3},{4,5},{5,6},{6,7},{8,9},{9,10},{10,11},{12,13},{... | collective-permute-start | bytes 294920 | tf_op jit(solution)/shard_map/ppermute | solution.py:238
  5.6 4.0 %head.1 = (bf16[2,512,768]{2,1,0:T(8,128)(2,1)S(1)}, bf16[2,256,768]{2,1,0:T(8,128)(2,1)S(1)}, f32[2,512,256]{2,1,0:T(8,128)S(1)}, f32[8,8,2048]{2,1,0:T(8,128)S(1)}, bf16[2,1024,768]{2,1,0:T(8,128)(2,1)S(1)}) custom-call(s32[768]{0:T(1024)} %owner_hbm.1, bf16[8,32,2048]{2,1,0:T(8,128)(2,1)} %x_hbm.1, f32[4,2048]{1,0:T(4,128)} %w_ref.1, ...), custom_call_target="tpu_custom_call" | custom-call | flops 150994944 | bytes 8388608 | tf_op jit(solution)/shard_map/head/pallas_call | solution.py:239
  9.6 0.0 collective-permute-done.prev_ref
  9.6 0.0 copy-done
  9.7 1.8 %spectra.1 = bf16[4096,128]{1,0:T(8,128)(2,1)S(1)} custom-call(bf16[8,3,2048]{2,1,0:T(4,128)(2,1)S(1)} %collective-permute-done.prev_ref, f32[4,2048]{1,0:T(4,128)S(1)} %copy-done, bf16[2,512,768]{2,1,0:T(8,128)(2,1)S(1)} %get-tuple-element.7.pick_ref, bf16[2,256,768]{2,1,0:T(8,128)(2,1)S(1)} %get-tuple-element.8.spec_in, ...), custom_call_target="tpu_custom_call" | custom-call | flops 805306368 | bytes 8388608 | tf_op jit(solution)/shard_map/spectra/pallas_call | solution.py:264
  11.4 53.4 %all_to_all.9 = bf16[512,8,128]{2,1,0:T(8,128)(2,1)S(1)} all-to-all(bf16[512,8,128]{2,1,0:T(8,128)(2,1)S(1)} %bitcast.3), channel_id=1, replica_groups=mesh['inp'=128,'sec'=4] {'sec','inp'}, dimensions={0} | all-to-all | bytes 2097152 | tf_op jit(solution)/shard_map/all_to_all | solution.py:280
  64.9 2.8 %cross.1 = (bf16[2,1024,1024]{2,1,0:T(8,128)(2,1)}, f32[2,1024]{1,0:T(2,128)}) custom-call(bf16[4,1024,128]{2,1,0:T(8,128)(2,1)S(1)} %bitcast.2), custom_call_target="tpu_custom_call" | custom-call | tf_op jit(solution)/shard_map/cross/pallas_call | solution.py:281
Async XLA Ops:
  0.6 9.0 %copy-start = (f32[4,2048]{1,0:T(4,128)S(1)}, f32[4,2048]{1,0:T(4,128)}, u32[]{:S(2)}) copy-start(f32[4,2048]{1,0:T(4,128)} %w_ref.1) | copy-start | bytes 98308
  1.7 8.0 %collective-permute-start = (bf16[8,3,2048]{2,1,0:T(4,128)(2,1)S(1)}, bf16[8,3,2048]{2,1,0:T(4,128)(2,1)S(1)}, u32[]{:S(2)}, u32[]{:S(2)}) collective-permute-start(bf16[8,3,2048]{2,1,0:T(4,128)(2,1)S(1)} %slice.3), channel_id=1, source_target_pairs={{0,1},{1,2},{2,3},{4,5},{5,6},{6,7},{8,9},{9,10},{10,11},{12,13},{... | collective-permute-start | bytes 294920 | tf_op jit(solution)/shard_map/ppermute | solution.py:238

commit v9 on v8

--- a/solution.py
+++ b/solution.py
@@ -126,11 +126,16 @@
 def spectra_kernel(
     prev_ref, w_ref, pick_ref, spec_in, late_ref, edge_ref, tab_ref, out_ref, ext, filt, spec, early, rows
 ):
-    ext[:, EDGE - (TAPS - 1) :, :] = prev_ref[...].astype(jnp.float32)
+    for k in range(TAPS - 1):
+        frames = prev_ref[k].astype(jnp.float32)
+        for tile in range(POINTS // 128):
+            at = pl.ds(EDGE - (TAPS - 1) + k, IN_DEV, stride=EDGE)
+            ext[tile, at, :] = frames[:, tile * 128 : (tile + 1) * 128]
     frame = lax.broadcasted_iota(jnp.int32, (EDGE, HALF), 0)
 
     def fir(i, lanes):
-        halo = ext[i, :, lanes]
+        span = slice(i * EDGE, (i + 1) * EDGE)
+        halo = jnp.concatenate([ext[tile, span, :] for tile in range(lanes.start // 128, lanes.stop // 128)], axis=1)
         total = edge_ref[i, :, lanes]
         for tap in range(1, TAPS):
             total = total + jnp.where(frame < tap, w_ref[tap : tap + 1, lanes] * pltpu.roll(halo, tap, 0), 0.0)
@@ -234,7 +239,7 @@
 
 
 def local(samples, fir_weights, channel_owner):
-    last_frames = samples[:, FR_DEV - (TAPS - 1) :, :]
+    last_frames = samples[:, FR_DEV - (TAPS - 1) :, :].transpose(1, 0, 2)
     previous = lax.ppermute(last_frames, "sec", [(i, i + 1) for i in range(SECS - 1)])
     pick, spectra, late, edge, table = pl.pallas_call(
         head_kernel,
@@ -267,7 +272,7 @@
         in_specs=[VMEM] * 7,
         out_specs=VMEM,
         scratch_shapes=[
-            pltpu.VMEM((IN_DEV, EDGE, POINTS), jnp.float32),
+            pltpu.VMEM((POINTS // 128, IN_DEV * EDGE + EDGE, 128), jnp.float32),
             pltpu.VMEM((2, IN_DEV * REDO, HALF), jnp.bfloat16),
             pltpu.VMEM((2, ROWS, CHANNELS), jnp.bfloat16),
             pltpu.VMEM((2, DEVS, ROWS), jnp.float32),

time: 67.9 us -> 67.9 us (level)
  no operation moved by 1% of the time
where the time goes in v9:
time: 67.9 us; the launch traced here: 67.7 us
  blocking collectives  53.4 us (79%)
  Pallas kernels  8.55 us (13%)
  starting transfers between devices  3.95 us (6%)
  local copies, waits for them, and re-layouts  1.11 us (2%)
  between operations  0.68 us (1%)
    all_to_all x1, blocking collectives, local(): lax.all_to_all(buffer, ('sec', 'inp'), split_axis=0, concat_axis=0, tiled...  53.4 us
    pallas_call x1, Pallas kernels, local(): pl.pallas_call(head_kernel, out_shape=(shaped(2, DEVS, CHANNELS), shaped(...  3.99 us
    ppermute x1, starting transfers between devices, local(): lax.ppermute(last_frames, 'sec', [(i, i + 1) for i in range(SECS - 1)])  3.95 us
    pallas_call x1, Pallas kernels, local(): pl.pallas_call(cross_kernel, out_shape=(shaped(2, INPUTS, INPUTS), shaped...  2.83 us
    pallas_call x1, Pallas kernels, local(): pl.pallas_call(spectra_kernel, out_shape=shaped(DEVS * IN_DEV, 128), in_s...  1.73 us
  transfers between devices with their start and end apart: 1, of which 0 were waited for; matrix products, arithmetic and copies ran while one was open for 0% of the time, Pallas kernels for 6%

profile of v9, /device:TPU:1, one launch (start us, length us, event | category | flops | bytes accessed | tf_op | source)
XLA Modules:
  0.0 67.7 jit_solution(10184337841172680412)
XLA Ops:
  0.6 0.0 copy-start
  0.6 1.0 %slice.3 = bf16[8,3,2048]{2,1,0:T(4,128)(2,1)S(1)} slice(bf16[8,32,2048]{2,1,0:T(8,128)(2,1)} %x_hbm.1), slice={[0:8], [29:32], [0:2048]} | slice | bytes 196608 | tf_op jit(solution)/shard_map/slice | solution.py:242
  1.7 0.1 copy.9
  1.8 4.0 %collective-permute-start = (bf16[3,8,2048]{2,1,0:T(8,128)(2,1)S(1)}, bf16[3,8,2048]{2,1,0:T(8,128)(2,1)S(1)}, u32[]{:S(2)}, u32[]{:S(2)}) collective-permute-start(bf16[3,8,2048]{2,1,0:T(8,128)(2,1)S(1)} %bitcast.7), channel_id=1, source_target_pairs={{0,1},{1,2},{2,3},{4,5},{5,6},{6,7},{8,9},{9,10},{10,11},{12,13},{... | collective-permute-start | bytes 294920 | tf_op jit(solution)/shard_map/ppermute | solution.py:243
  5.7 4.0 %head.1 = (bf16[2,512,768]{2,1,0:T(8,128)(2,1)S(1)}, bf16[2,256,768]{2,1,0:T(8,128)(2,1)S(1)}, f32[2,512,256]{2,1,0:T(8,128)S(1)}, f32[8,8,2048]{2,1,0:T(8,128)S(1)}, bf16[2,1024,768]{2,1,0:T(8,128)(2,1)S(1)}) custom-call(s32[768]{0:T(1024)} %owner_hbm.1, bf16[8,32,2048]{2,1,0:T(8,128)(2,1)} %x_hbm.1, f32[4,2048]{1,0:T(4,128)} %w_ref.1, ...), custom_call_target="tpu_custom_call" | custom-call | flops 150994944 | bytes 8388608 | tf_op jit(solution)/shard_map/head/pallas_call | solution.py:244
  9.7 0.0 collective-permute-done.prev_ref
  9.7 0.0 copy-done
  9.7 1.7 %spectra.1 = bf16[4096,128]{1,0:T(8,128)(2,1)S(1)} custom-call(bf16[3,8,2048]{2,1,0:T(8,128)(2,1)S(1)} %collective-permute-done.prev_ref, f32[4,2048]{1,0:T(4,128)S(1)} %copy-done, bf16[2,512,768]{2,1,0:T(8,128)(2,1)S(1)} %get-tuple-element.7.pick_ref, bf16[2,256,768]{2,1,0:T(8,128)(2,1)S(1)} %get-tuple-element.8.spec_in, ...), custom_call_target="tpu_custom_call" | custom-call | flops 805306368 | bytes 8388608 | tf_op jit(solution)/shard_map/spectra/pallas_call | solution.py:269
  11.5 53.4 %all_to_all.9 = bf16[512,8,128]{2,1,0:T(8,128)(2,1)S(1)} all-to-all(bf16[512,8,128]{2,1,0:T(8,128)(2,1)S(1)} %bitcast.6), channel_id=1, replica_groups=mesh['inp'=128,'sec'=4] {'sec','inp'}, dimensions={0} | all-to-all | bytes 2097152 | tf_op jit(solution)/shard_map/all_to_all | solution.py:285
  64.9 2.8 %cross.1 = (bf16[2,1024,1024]{2,1,0:T(8,128)(2,1)}, f32[2,1024]{1,0:T(2,128)}) custom-call(bf16[4,1024,128]{2,1,0:T(8,128)(2,1)S(1)} %bitcast.5), custom_call_target="tpu_custom_call" | custom-call | tf_op jit(solution)/shard_map/cross/pallas_call | solution.py:286
Async XLA Ops:
  0.6 9.1 %copy-start = (f32[4,2048]{1,0:T(4,128)S(1)}, f32[4,2048]{1,0:T(4,128)}, u32[]{:S(2)}) copy-start(f32[4,2048]{1,0:T(4,128)} %w_ref.1) | copy-start | bytes 98308
  1.8 8.0 %collective-permute-start = (bf16[3,8,2048]{2,1,0:T(8,128)(2,1)S(1)}, bf16[3,8,2048]{2,1,0:T(8,128)(2,1)S(1)}, u32[]{:S(2)}, u32[]{:S(2)}) collective-permute-start(bf16[3,8,2048]{2,1,0:T(8,128)(2,1)S(1)} %bitcast.7), channel_id=1, source_target_pairs={{0,1},{1,2},{2,3},{4,5},{5,6},{6,7},{8,9},{9,10},{10,11},{12,13},{... | collective-permute-start | bytes 294920 | tf_op jit(solution)/shard_map/ppermute | solution.py:243

commit v10 on v9

--- a/solution.py
+++ b/solution.py
@@ -54,11 +54,10 @@
     named = (lax.broadcasted_iota(jnp.int32, (OWNERS, CHANNELS), 0) == owner).astype(jnp.float32)
     counts = jnp.dot(named.astype(jnp.bfloat16), earlier, preferred_element_type=jnp.float32)
     rank = jnp.sum(counts * named, axis=0, keepdims=True).astype(jnp.int32)
-    target = ((rank >> 1) * OWNERS + owner) * 2 + (rank & 1)
-    target = jnp.where(rank < 2 * SECS, target, -1)
+    device = jnp.where(rank < 2 * SECS, (rank >> 1) * OWNERS + owner, -1)
+    place = lax.broadcasted_iota(jnp.int32, (DEVS, CHANNELS), 0)
     for side in range(2):
-        place = 2 * lax.broadcasted_iota(jnp.int32, (DEVS, CHANNELS), 0) + side
-        pick_ref[side] = as_bf16(place == target)
+        pick_ref[side] = as_bf16(place == jnp.where((rank & 1) == side, device, -1))
 
 
 def transform(rows, table):

time: 67.9 us -> 68 us (level)
  no operation moved by 1% of the time
where the time goes in v10:
time: 68 us; the launch traced here: 67.9 us
  blocking collectives  53.5 us (79%)
  Pallas kernels  8.66 us (13%)
  starting transfers between devices  3.95 us (6%)
  local copies, waits for them, and re-layouts  1.11 us (2%)
  between operations  0.68 us (1%)
    all_to_all x1, blocking collectives, local(): lax.all_to_all(buffer, ('sec', 'inp'), split_axis=0, concat_axis=0, tiled...  53.5 us
    pallas_call x1, Pallas kernels, local(): pl.pallas_call(head_kernel, out_shape=(shaped(2, DEVS, CHANNELS), shaped(...  4.1 us
    ppermute x1, starting transfers between devices, local(): lax.ppermute(last_frames, 'sec', [(i, i + 1) for i in range(SECS - 1)])  3.95 us
    pallas_call x1, Pallas kernels, local(): pl.pallas_call(cross_kernel, out_shape=(shaped(2, INPUTS, INPUTS), shaped...  2.83 us
    pallas_call x1, Pallas kernels, local(): pl.pallas_call(spectra_kernel, out_shape=shaped(DEVS * IN_DEV, 128), in_s...  1.73 us
  transfers between devices with their start and end apart: 1, of which 0 were waited for; matrix products, arithmetic and copies ran while one was open for 0% of the time, Pallas kernels for 6%

profile of v10, /device:TPU:1, one launch (start us, length us, event | category | flops | bytes accessed | tf_op | source)
XLA Modules:
  0.0 67.9 jit_solution(17655210257703761957)
XLA Ops:
  0.6 0.0 copy-start
  0.6 1.0 %slice.3 = bf16[8,3,2048]{2,1,0:T(4,128)(2,1)S(1)} slice(bf16[8,32,2048]{2,1,0:T(8,128)(2,1)} %x_hbm.1), slice={[0:8], [29:32], [0:2048]} | slice | bytes 196608 | tf_op jit(solution)/shard_map/slice | solution.py:241
  1.7 0.1 copy.9
  1.8 4.0 %collective-permute-start = (bf16[3,8,2048]{2,1,0:T(8,128)(2,1)S(1)}, bf16[3,8,2048]{2,1,0:T(8,128)(2,1)S(1)}, u32[]{:S(2)}, u32[]{:S(2)}) collective-permute-start(bf16[3,8,2048]{2,1,0:T(8,128)(2,1)S(1)} %bitcast.7), channel_id=1, source_target_pairs={{0,1},{1,2},{2,3},{4,5},{5,6},{6,7},{8,9},{9,10},{10,11},{12,13},{... | collective-permute-start | bytes 294920 | tf_op jit(solution)/shard_map/ppermute | solution.py:242
  5.7 4.1 %head.1 = (bf16[2,512,768]{2,1,0:T(8,128)(2,1)S(1)}, bf16[2,256,768]{2,1,0:T(8,128)(2,1)S(1)}, f32[2,512,256]{2,1,0:T(8,128)S(1)}, f32[8,8,2048]{2,1,0:T(8,128)S(1)}, bf16[2,1024,768]{2,1,0:T(8,128)(2,1)S(1)}) custom-call(s32[768]{0:T(1024)} %owner_hbm.1, bf16[8,32,2048]{2,1,0:T(8,128)(2,1)} %x_hbm.1, f32[4,2048]{1,0:T(4,128)} %w_ref.1, ...), custom_call_target="tpu_custom_call" | custom-call | flops 150994944 | bytes 8388608 | tf_op jit(solution)/shard_map/head/pallas_call | solution.py:243
  9.8 0.0 collective-permute-done.prev_ref
  9.8 0.0 copy-done
  9.8 1.7 %spectra.1 = bf16[4096,128]{1,0:T(8,128)(2,1)S(1)} custom-call(bf16[3,8,2048]{2,1,0:T(8,128)(2,1)S(1)} %collective-permute-done.prev_ref, f32[4,2048]{1,0:T(4,128)S(1)} %copy-done, bf16[2,512,768]{2,1,0:T(8,128)(2,1)S(1)} %get-tuple-element.7.pick_ref, bf16[2,256,768]{2,1,0:T(8,128)(2,1)S(1)} %get-tuple-element.8.spec_in, ...), custom_call_target="tpu_custom_call" | custom-call | flops 805306368 | bytes 8388608 | tf_op jit(solution)/shard_map/spectra/pallas_call | solution.py:268
  11.6 53.5 %all_to_all.9 = bf16[512,8,128]{2,1,0:T(8,128)(2,1)S(1)} all-to-all(bf16[512,8,128]{2,1,0:T(8,128)(2,1)S(1)} %bitcast.6), channel_id=1, replica_groups=mesh['inp'=128,'sec'=4] {'sec','inp'}, dimensions={0} | all-to-all | bytes 2097152 | tf_op jit(solution)/shard_map/all_to_all | solution.py:284
  65.0 2.8 %cross.1 = (bf16[2,1024,1024]{2,1,0:T(8,128)(2,1)}, f32[2,1024]{1,0:T(2,128)}) custom-call(bf16[4,1024,128]{2,1,0:T(8,128)(2,1)S(1)} %bitcast.5), custom_call_target="tpu_custom_call" | custom-call | tf_op jit(solution)/shard_map/cross/pallas_call | solution.py:285
Async XLA Ops:
  0.6 9.2 %copy-start = (f32[4,2048]{1,0:T(4,128)S(1)}, f32[4,2048]{1,0:T(4,128)}, u32[]{:S(2)}) copy-start(f32[4,2048]{1,0:T(4,128)} %w_ref.1) | copy-start | bytes 98308
  1.8 8.1 %collective-permute-start = (bf16[3,8,2048]{2,1,0:T(8,128)(2,1)S(1)}, bf16[3,8,2048]{2,1,0:T(8,128)(2,1)S(1)}, u32[]{:S(2)}, u32[]{:S(2)}) collective-permute-start(bf16[3,8,2048]{2,1,0:T(8,128)(2,1)S(1)} %bitcast.7), channel_id=1, source_target_pairs={{0,1},{1,2},{2,3},{4,5},{5,6},{6,7},{8,9},{9,10},{10,11},{12,13},{... | collective-permute-start | bytes 294920 | tf_op jit(solution)/shard_map/ppermute | solution.py:242
